TPU v7x, 128 devices: a whole 4x4x4 slice. The times are simulated.
128 devices in a mesh: rep: 4 (over z_lo, core), fsdp: 32 (over x, z_hi, y).
Axes of the slice: x: 4, y: 4, z: 4 (z_hi: 2, z_lo: 2; z = z_hi * 2 + z_lo), core: 2. Of those that a mesh axis runs over, the one named last changes fastest.
Arguments:
- tokens: bfloat16 [65536, 768], P(('rep', 'fsdp')), may hold values from -6 to 6
- image_lengths: int32 [128, 6], P(('rep', 'fsdp')), may hold values from 1 to 256, 512 in all within a row
- pad_counts: int32 [128], P(('rep', 'fsdp')), may hold values from 0 to 127
- out_grad: bfloat16 [65536, 768], P(('rep', 'fsdp')), may hold values from -6 to 6
- first_gain: bfloat16 [768], P('fsdp'), may hold values from 0.25 to 1.75
- first_shift: bfloat16 [768], P('fsdp'), may hold values from -2 to 2
- input_weight: bfloat16 [768, 2304], P('fsdp'), may hold values from -0.21875 to 0.21875
- query_bias: bfloat16 [768], P('fsdp'), may hold values from -2 to 2
- value_bias: bfloat16 [768], P('fsdp'), may hold values from -2 to 2
- output_weight: bfloat16 [768, 768], P('fsdp'), may hold values from -2 to 2
- output_bias: bfloat16 [768], P('fsdp'), may hold values from -2 to 2
- second_gain: bfloat16 [768], P('fsdp'), may hold values from 0.25 to 1.75
- second_shift: bfloat16 [768], P('fsdp'), may hold values from -2 to 2
- up_weight: bfloat16 [768, 3072], P('fsdp'), may hold values from -0.21875 to 0.21875
- up_bias: bfloat16 [3072], P('fsdp'), may hold values from -2 to 2
- down_weight: bfloat16 [3072, 768], P('fsdp'), may hold values from -0.109375 to 0.109375
- down_bias: bfloat16 [768], P('fsdp'), may hold values from -2 to 2
Outputs:
- layer_out: bfloat16 [65536, 768], P(('rep', 'fsdp'))
- input_grad: float32 [65536, 768], P(('rep', 'fsdp'))
- first_gain_gradient: float32 [768], P('fsdp')
- first_shift_gradient: float32 [768], P('fsdp')
- input_weight_gradient: float32 [768, 2304], P('fsdp')
- query_bias_gradient: float32 [768], P('fsdp')
- value_bias_gradient: float32 [768], P('fsdp')
- output_weight_gradient: float32 [768, 768], P('fsdp')
- output_bias_gradient: float32 [768], P('fsdp')
- second_gain_gradient: float32 [768], P('fsdp')
- second_shift_gradient: float32 [768], P('fsdp')
- up_weight_gradient: float32 [768, 3072], P('fsdp')
- up_bias_gradient: float32 [3072], P('fsdp')
- down_weight_gradient: float32 [3072, 768], P('fsdp')
- down_bias_gradient: float32 [768], P('fsdp')
Inputs may be any that keep to these rules, and one draw needn't show every extreme that they name: `image_lengths`: each row sums to 512, and the largest image of each row has 256 patches.
All inputs are finite; a program needn't handle non-finite values.
Results may differ from a plain program's by a relative error of at most 0.025.
Values may be sent and summed in bfloat16 or wider, within the bound.
A program may use at most 128 MiB of HBM per device.

v0:
```python
import jax
import jax.numpy as jnp
from jax import lax
from jax.sharding import PartitionSpec as P

HEAD = 64


EPSILON = 1e-06


def sequence_mask(lengths_row, padding, length):
    positions = jnp.arange(length, dtype=jnp.int32)
    starts = jnp.cumsum(lengths_row) - lengths_row
    segment = jnp.sum((positions[:, None] >= starts[None, :]).astype(jnp.int32), axis=1)
    valid = positions < length - padding
    same = (segment[:, None] == segment[None, :]) & valid[:, None] & valid[None, :]
    return same | (positions[:, None] == positions[None, :])


def normalize(values):
    average = jnp.mean(values, axis=1, keepdims=True)
    centred = values - average
    inv_spread = lax.rsqrt(jnp.mean(centred * centred, axis=1, keepdims=True) + EPSILON)
    return (centred * inv_spread, inv_spread)


def norm_backward(grad_rows, normed, inv_spread, gain):
    scaled = grad_rows * gain
    centre = jnp.mean(scaled, axis=1, keepdims=True)
    along = jnp.mean(scaled * normed, axis=1, keepdims=True)
    return inv_spread * (scaled - centre - normed * along)


def transposed(left, right):
    return lax.dot_general(
        left, right, (((0,), (0,)), ((), ())), preferred_element_type=jnp.float32
    )


def against(left, right):
    return lax.dot_general(
        left, right, (((1,), (1,)), ((), ())), preferred_element_type=jnp.float32
    )


def column_sum(values):
    return jnp.sum(values.astype(jnp.float32), axis=0)


def split_heads(block, heads):
    return block.reshape(block.shape[0], heads, block.shape[1] // heads)


def masked_scores(queries, keys, allowed):
    scores = jnp.einsum(
        "qhd,khd->hqk", queries, keys, preferred_element_type=jnp.float32
    ) * HEAD ** (-0.5)
    return jnp.where(allowed[None], scores, -1e30)


def shards(
    tokens,
    image_lengths,
    pad_counts,
    out_grad,
    first_gain,
    first_shift,
    input_weight,
    query_bias,
    value_bias,
    output_weight,
    output_bias,
    second_gain,
    second_shift,
    up_weight,
    up_bias,
    down_weight,
    down_bias,
):
    floats = jnp.float32
    halves = jnp.bfloat16
    length, width = tokens.shape
    heads = width // HEAD
    allowed = sequence_mask(image_lengths[0], pad_counts[0], length)
    attn_shards = (
        first_gain,
        first_shift,
        input_weight,
        query_bias,
        value_bias,
        output_weight,
        output_bias,
    )
    mlp_shards = (second_gain, second_shift, up_weight, up_bias, down_weight, down_bias)
    attn_full = (
        lax.all_gather(attn_shards[0], "fsdp", axis=0, tiled=True),
        lax.all_gather(attn_shards[1], "fsdp", axis=0, tiled=True),
        lax.all_gather(attn_shards[2], "fsdp", axis=0, tiled=True),
        lax.all_gather(attn_shards[3], "fsdp", axis=0, tiled=True),
        lax.all_gather(attn_shards[4], "fsdp", axis=0, tiled=True),
        lax.all_gather(attn_shards[5], "fsdp", axis=0, tiled=True),
        lax.all_gather(attn_shards[6], "fsdp", axis=0, tiled=True),
    )
    gain_one, shift_one, joint_weight, bias_query, bias_value, proj_weight, proj_bias = attn_full
    inputs = tokens.astype(floats)
    normed_one, spread_one = normalize(inputs)
    hidden_one = (normed_one * gain_one.astype(floats) + shift_one.astype(floats)).astype(halves)
    joint_bias = jnp.concatenate([bias_query, jnp.zeros_like(bias_query), bias_value]).astype(
        floats
    )
    joint = (jnp.dot(hidden_one, joint_weight, preferred_element_type=floats) + joint_bias).astype(
        halves
    )
    queries = split_heads(joint[:, :width], heads)
    keys = split_heads(joint[:, width : 2 * width], heads)
    values = split_heads(joint[:, 2 * width :], heads)
    scores = masked_scores(queries, keys, allowed)
    highest = jnp.max(scores, axis=2, keepdims=True)
    log_total = highest + jnp.log(jnp.sum(jnp.exp(scores - highest), axis=2, keepdims=True))
    weights_low = jnp.exp(scores - log_total).astype(halves)
    attended = (
        jnp.einsum("hqk,khd->qhd", weights_low, values, preferred_element_type=floats)
        .reshape(length, width)
        .astype(halves)
    )
    residual = (
        inputs
        + jnp.dot(attended, proj_weight, preferred_element_type=floats)
        + proj_bias.astype(floats)
    )
    mlp_full = (
        lax.all_gather(mlp_shards[0], "fsdp", axis=0, tiled=True),
        lax.all_gather(mlp_shards[1], "fsdp", axis=0, tiled=True),
        lax.all_gather(mlp_shards[2], "fsdp", axis=0, tiled=True),
        lax.all_gather(mlp_shards[3], "fsdp", axis=0, tiled=True),
        lax.all_gather(mlp_shards[4], "fsdp", axis=0, tiled=True),
        lax.all_gather(mlp_shards[5], "fsdp", axis=0, tiled=True),
    )
    gain_two, shift_two, weight_up, bias_up, weight_down, bias_down = mlp_full
    normed_two, spread_two = normalize(residual)
    hidden_two = (normed_two * gain_two.astype(floats) + shift_two.astype(floats)).astype(halves)
    pre_act = jnp.dot(hidden_two, weight_up, preferred_element_type=floats) + bias_up.astype(floats)
    activated = jax.nn.gelu(pre_act).astype(halves)
    layer_out = (
        residual
        + jnp.dot(activated, weight_down, preferred_element_type=floats)
        + bias_down.astype(floats)
    ).astype(halves)
    mlp_back = (
        lax.all_gather(mlp_shards[0], "fsdp", axis=0, tiled=True),
        lax.all_gather(mlp_shards[1], "fsdp", axis=0, tiled=True),
        lax.all_gather(mlp_shards[2], "fsdp", axis=0, tiled=True),
        lax.all_gather(mlp_shards[3], "fsdp", axis=0, tiled=True),
        lax.all_gather(mlp_shards[4], "fsdp", axis=0, tiled=True),
        lax.all_gather(mlp_shards[5], "fsdp", axis=0, tiled=True),
    )
    gain_two, shift_two, weight_up, bias_up, weight_down, bias_down = mlp_back
    upstream = out_grad.astype(floats)
    grad_down = transposed(activated, out_grad)
    grad_bias_down = column_sum(out_grad)
    grad_act = against(out_grad, weight_down)
    unused, gelu_back = jax.vjp(jax.nn.gelu, pre_act)
    grad_pre = gelu_back(grad_act)[0].astype(halves)
    grad_up = transposed(hidden_two, grad_pre)
    grad_bias_up = column_sum(grad_pre)
    grad_hidden_two = against(grad_pre, weight_up)
    grad_gain_two = jnp.sum(grad_hidden_two * normed_two, axis=0)
    grad_shift_two = jnp.sum(grad_hidden_two, axis=0)
    grad_residual = upstream + norm_backward(
        grad_hidden_two, normed_two, spread_two, gain_two.astype(floats)
    )
    mlp_local = (grad_gain_two, grad_shift_two, grad_up, grad_bias_up, grad_down, grad_bias_down)
    mlp_part = (
        lax.psum_scatter(
            mlp_local[0].astype(jnp.bfloat16), "fsdp", scatter_dimension=0, tiled=True
        ).astype(jnp.float32),
        lax.psum_scatter(
            mlp_local[1].astype(jnp.bfloat16), "fsdp", scatter_dimension=0, tiled=True
        ).astype(jnp.float32),
        lax.psum_scatter(
            mlp_local[2].astype(jnp.bfloat16), "fsdp", scatter_dimension=0, tiled=True
        ).astype(jnp.float32),
        lax.psum_scatter(
            mlp_local[3].astype(jnp.bfloat16), "fsdp", scatter_dimension=0, tiled=True
        ).astype(jnp.float32),
        lax.psum_scatter(
            mlp_local[4].astype(jnp.bfloat16), "fsdp", scatter_dimension=0, tiled=True
        ).astype(jnp.float32),
        lax.psum_scatter(
            mlp_local[5].astype(jnp.bfloat16), "fsdp", scatter_dimension=0, tiled=True
        ).astype(jnp.float32),
    )
    mlp_done = (
        lax.psum(mlp_part[0].astype(jnp.bfloat16), "rep").astype(jnp.float32),
        lax.psum(mlp_part[1].astype(jnp.bfloat16), "rep").astype(jnp.float32),
        lax.psum(mlp_part[2].astype(jnp.bfloat16), "rep").astype(jnp.float32),
        lax.psum(mlp_part[3].astype(jnp.bfloat16), "rep").astype(jnp.float32),
        lax.psum(mlp_part[4].astype(jnp.bfloat16), "rep").astype(jnp.float32),
        lax.psum(mlp_part[5].astype(jnp.bfloat16), "rep").astype(jnp.float32),
    )
    attn_back = (
        lax.all_gather(attn_shards[0], "fsdp", axis=0, tiled=True),
        lax.all_gather(attn_shards[1], "fsdp", axis=0, tiled=True),
        lax.all_gather(attn_shards[2], "fsdp", axis=0, tiled=True),
        lax.all_gather(attn_shards[3], "fsdp", axis=0, tiled=True),
        lax.all_gather(attn_shards[4], "fsdp", axis=0, tiled=True),
        lax.all_gather(attn_shards[5], "fsdp", axis=0, tiled=True),
        lax.all_gather(attn_shards[6], "fsdp", axis=0, tiled=True),
    )
    gain_one, shift_one, joint_weight, bias_query, bias_value, proj_weight, proj_bias = attn_back
    grad_branch = grad_residual.astype(halves)
    grad_proj = transposed(attended, grad_branch)
    grad_proj_bias = column_sum(grad_branch)
    grad_attended = split_heads(against(grad_branch, proj_weight).astype(halves), heads)
    weights = jnp.exp(masked_scores(queries, keys, allowed) - log_total)
    grad_values = jnp.einsum(
        "hqk,qhd->khd", weights.astype(halves), grad_attended, preferred_element_type=floats
    )
    grad_weights = jnp.einsum("qhd,khd->hqk", grad_attended, values, preferred_element_type=floats)
    grad_scores = (
        weights * (grad_weights - jnp.sum(grad_weights * weights, axis=2, keepdims=True))
    ).astype(halves)
    grad_queries = jnp.einsum(
        "hqk,khd->qhd", grad_scores, keys, preferred_element_type=floats
    ) * HEAD ** (-0.5)
    grad_keys = jnp.einsum(
        "hqk,qhd->khd", grad_scores, queries, preferred_element_type=floats
    ) * HEAD ** (-0.5)
    grad_joint = jnp.concatenate(
        [
            grad_queries.reshape(length, width),
            grad_keys.reshape(length, width),
            grad_values.reshape(length, width),
        ],
        axis=1,
    ).astype(halves)
    grad_joint_weight = transposed(hidden_one, grad_joint)
    grad_query = column_sum(grad_joint[:, :width])
    grad_value = column_sum(grad_joint[:, 2 * width :])
    grad_hidden_one = against(grad_joint, joint_weight)
    grad_gain_one = jnp.sum(grad_hidden_one * normed_one, axis=0)
    grad_shift_one = jnp.sum(grad_hidden_one, axis=0)
    input_grad = grad_residual + norm_backward(
        grad_hidden_one, normed_one, spread_one, gain_one.astype(floats)
    )
    attn_local = (
        grad_gain_one,
        grad_shift_one,
        grad_joint_weight,
        grad_query,
        grad_value,
        grad_proj,
        grad_proj_bias,
    )
    attn_part = (
        lax.psum_scatter(
            attn_local[0].astype(jnp.bfloat16), "fsdp", scatter_dimension=0, tiled=True
        ).astype(jnp.float32),
        lax.psum_scatter(
            attn_local[1].astype(jnp.bfloat16), "fsdp", scatter_dimension=0, tiled=True
        ).astype(jnp.float32),
        lax.psum_scatter(
            attn_local[2].astype(jnp.bfloat16), "fsdp", scatter_dimension=0, tiled=True
        ).astype(jnp.float32),
        lax.psum_scatter(
            attn_local[3].astype(jnp.bfloat16), "fsdp", scatter_dimension=0, tiled=True
        ).astype(jnp.float32),
        lax.psum_scatter(
            attn_local[4].astype(jnp.bfloat16), "fsdp", scatter_dimension=0, tiled=True
        ).astype(jnp.float32),
        lax.psum_scatter(
            attn_local[5].astype(jnp.bfloat16), "fsdp", scatter_dimension=0, tiled=True
        ).astype(jnp.float32),
        lax.psum_scatter(
            attn_local[6].astype(jnp.bfloat16), "fsdp", scatter_dimension=0, tiled=True
        ).astype(jnp.float32),
    )
    attn_done = (
        lax.psum(attn_part[0].astype(jnp.bfloat16), "rep").astype(jnp.float32),
        lax.psum(attn_part[1].astype(jnp.bfloat16), "rep").astype(jnp.float32),
        lax.psum(attn_part[2].astype(jnp.bfloat16), "rep").astype(jnp.float32),
        lax.psum(attn_part[3].astype(jnp.bfloat16), "rep").astype(jnp.float32),
        lax.psum(attn_part[4].astype(jnp.bfloat16), "rep").astype(jnp.float32),
        lax.psum(attn_part[5].astype(jnp.bfloat16), "rep").astype(jnp.float32),
        lax.psum(attn_part[6].astype(jnp.bfloat16), "rep").astype(jnp.float32),
    )
    return (
        layer_out,
        input_grad,
        attn_done[0],
        attn_done[1],
        attn_done[2],
        attn_done[3],
        attn_done[4],
        attn_done[5],
        attn_done[6],
        mlp_done[0],
        mlp_done[1],
        mlp_done[2],
        mlp_done[3],
        mlp_done[4],
        mlp_done[5],
    )


def solution(mesh):
    return jax.shard_map(
        shards,
        mesh=mesh,
        in_specs=(
            P(("rep", "fsdp"), None),
            P(("rep", "fsdp"), None),
            P(("rep", "fsdp")),
            P(("rep", "fsdp"), None),
            P("fsdp"),
            P("fsdp"),
            P("fsdp", None),
            P("fsdp"),
            P("fsdp"),
            P("fsdp", None),
            P("fsdp"),
            P("fsdp"),
            P("fsdp"),
            P("fsdp", None),
            P("fsdp"),
            P("fsdp", None),
            P("fsdp"),
        ),
        out_specs=(
            P(("rep", "fsdp"), None),
            P(("rep", "fsdp"), None),
            P("fsdp"),
            P("fsdp"),
            P("fsdp", None),
            P("fsdp"),
            P("fsdp"),
            P("fsdp", None),
            P("fsdp"),
            P("fsdp"),
            P("fsdp"),
            P("fsdp", None),
            P("fsdp"),
            P("fsdp", None),
            P("fsdp"),
        ),
        check_vma=False,
    )
```

profile of v0, /device:TPU:1, one launch (start us, length us, event | category | flops | bytes accessed | tf_op | source)
XLA Modules:
  0.0 1353.4 jit_solution(15952248412285888327)
XLA Ops:
  20.0 158.3 %all-reduce.19 = (bf16[768]{0:T(1024)(128)(2,1)S(1)}, bf16[768]{0:T(1024)(128)(2,1)S(1)}, bf16[768]{0:T(1024)(128)(2,1)S(1)}, bf16[768]{0:T(1024)(128)(2,1)S(1)}...) all-reduce(bf16[768]{0:T(1024)(128)(2,1)S(1)} %dynamic-update-slice, ...), channel_id=1, replica_groups=mesh['rep'=4,'fsdp'=32] {'fsdp'}, use_global_device_ids=true, to_apply=%add.3 | all-reduce | flops 8448 | bytes 33792
  183.1 4.4 fusion.9
  188.6 2.1 fusion
  190.7 2.6 exponential_reduce_fusion
  193.3 2.0 copy-done
  195.2 4.3 convolution_convert_fusion.6
  199.6 3.5 fusion.44
  204.8 40.1 %all-gather.9.cloned.1.call-done = bf16[768,3072]{1,0:T(8,128)(2,1)} async-done(((bf16[24,3072]{1,0:T(8,128)(2,1)}), bf16[768,3072]{1,0:T(8,128)(2,1)}) %all-gather.9.cloned.1.call-update) | async-done | bytes 4718608 | tf_op jit(solution)/shard_map/all_gather | solution.py:135
  245.0 8.2 fusion.39
  253.2 76.6 %all-gather.11.cloned.1.call-done = bf16[3072,768]{1,0:T(8,128)(2,1)} async-done(((bf16[96,768]{1,0:T(8,128)(2,1)}), bf16[3072,768]{1,0:T(8,128)(2,1)}) %all-gather.11.cloned.1.call-update) | async-done | bytes 4718608 | tf_op jit(solution)/shard_map/all_gather | solution.py:137
  329.7 9.2 fusion.40
  338.9 5.6 multiply_reduce_fusion.1
  344.6 2.3 convert_reduce_fusion.2
  348.6 2.3 copy.64
  350.9 9.0 bitcast_reduce_fusion
  359.9 9.5 multiply_reduce_fusion
  369.5 7.2 multiply_convert_fusion
  376.6 2.0 multiply_convert_fusion.2
  380.8 4.1 convolution_convert_fusion.2
  385.0 7.4 convolution_convert_fusion.1
  393.5 8.6 convolution_convert_fusion
  402.2 3.0 convolution_convert_fusion.3
  407.2 6.1 fusion.22
  413.3 151.1 %all-reduce.18 = (bf16[768]{0:T(1024)(128)(2,1)S(1)}, bf16[768]{0:T(1024)(128)(2,1)S(1)}, bf16[768]{0:T(1024)(128)(2,1)S(1)}, bf16[768]{0:T(1024)(128)(2,1)S(1)}...) all-reduce(bf16[768]{0:T(1024)(128)(2,1)S(1)} %dynamic-update-slice, ...), channel_id=1, replica_groups=mesh['rep'=4,'fsdp'=32] {'fsdp'}, use_global_device_ids=true, to_apply=%add.8 | all-reduce | flops 9984 | bytes 39936
  564.4 9.4 add_convert_fusion
  573.9 35.1 %reduce-scatter.5.cloned.1.call-done = bf16[24,2304]{1,0:T(8,128)(2,1)} async-done(((bf16[768,2304]{1,0:T(8,128)(2,1)}), bf16[24,2304]{1,0:T(8,128)(2,1)}) %reduce-scatter.5.cloned.1.call-update) | async-done | bytes 110608 | tf_op jit(solution)/shard_map/reduce_scatter | solution.py:263
  608.9 233.6 %reduce-scatter.9.cloned.1.call-done = bf16[24,3072]{1,0:T(8,128)(2,1)} async-done(((bf16[768,3072]{1,0:T(8,128)(2,1)}), bf16[24,3072]{1,0:T(8,128)(2,1)}) %reduce-scatter.9.cloned.1.call-update) | async-done | bytes 147472 | tf_op jit(solution)/shard_map/reduce_scatter | solution.py:181
  842.5 233.7 %reduce-scatter.11.cloned.1.call-done = bf16[96,768]{1,0:T(8,128)(2,1)} async-done(((bf16[3072,768]{1,0:T(8,128)(2,1)}), bf16[96,768]{1,0:T(8,128)(2,1)}) %reduce-scatter.11.cloned.1.call-update) | async-done | bytes 147472 | tf_op jit(solution)/shard_map/reduce_scatter | solution.py:187
  1076.9 3.1 fusion.21
  1080.0 221.6 %reduce-scatter.7.cloned.1.call-done = bf16[24,768]{1,0:T(8,128)(2,1)} async-done(((bf16[768,768]{1,0:T(8,128)(2,1)}), bf16[24,768]{1,0:T(8,128)(2,1)}) %reduce-scatter.7.cloned.1.call-update) | async-done | bytes 36880 | tf_op jit(solution)/shard_map/reduce_scatter | solution.py:272
  1301.6 13.5 all-reduce.20
  1320.4 21.4 %all-reduce.24.cloned.1.call-done = (bf16[24,2304]{1,0:T(8,128)(2,1)}, bf16[24,3072]{1,0:T(8,128)(2,1)}, bf16[96,768]{1,0:T(8,128)(2,1)}) async-done(((bf16[24,2304]{1,0:T(8,128)(2,1)}, bf16[24,3072]{1,0:T(8,128)(2,1)}, bf16[96,768]{1,0:T(8,128)(2,1)}), (bf16[24,2304]{1,0:T(8,128)(2,1)}, bf16[24,3072]{1,0:T(8,128)(2,1)}, bf16[96,768]{1,0:T(8,128)(2,1)})) %all-reduce.24.cloned.1.call-update) | async-done | bytes 405520 | tf_op jit(solution)/shard_map/psum | solution.py:282
  (134 shorter events, 35.0 us)
Async XLA Ops:
  7.2 176.0 %all-gather.5.cloned.1.call-start = ((), (), s32[]{:S(2)}) async-start(), calls=%async_computation.4 | async-start | bytes 3649536 | tf_op jit(solution)/shard_map/all_gather | solution.py:99
  7.9 191.6 %all-gather.7.cloned.1.call-start = ((), (), s32[]{:S(2)}) async-start(), calls=%async_computation.5 | async-start | bytes 1216512 | tf_op jit(solution)/shard_map/all_gather | solution.py:102
  8.7 236.3 %all-gather.9.cloned.1.call-start = ((), (), s32[]{:S(2)}) async-start(), calls=%async_computation.6 | async-start | bytes 4866048 | tf_op jit(solution)/shard_map/all_gather | solution.py:135
  9.4 320.3 %all-gather.11.cloned.1.call-start = ((), (), s32[]{:S(2)}) async-start(), calls=%async_computation.7 | async-start | bytes 4866048 | tf_op jit(solution)/shard_map/all_gather | solution.py:137
  10.0 598.9 %reduce-scatter.5.cloned.1.call-start = ((), (), s32[]{:S(2)}) async-start(), calls=%async_computation.8 | async-start | bytes 3649536 | tf_op jit(solution)/shard_map/reduce_scatter | solution.py:263
  188.6 4.7 copy-start.3
  190.7 4.6 copy-start
  195.2 4.3 copy-start.1
  204.8 124.9 %copy-start.8 = (bf16[512,768]{1,0:T(8,128)(2,1)S(1)}, bf16[512,768]{1,0:T(8,128)(2,1)}, u32[]{:S(2)}) copy-start(bf16[512,768]{1,0:T(8,128)(2,1)} %param.20) | copy-start | bytes 2359300
  329.7 9.2 copy-start.12
  338.9 5.6 copy-start.16
  338.9 5.6 copy-start.9
  344.5 2.3 copy-start.13
  350.9 9.0 copy-start.4
  350.9 9.0 copy-start.5
  350.9 18.5 %slice-start = ((s8[12582912]{0:T(1024)(128)(4,1)}), s8[4194304]{0:T(1024)(128)(4,1)S(1)}, s32[]{:S(2)}) async-start(s8[12582912]{0:T(1024)(128)(4,1)} %bitcast.48), calls=%async_computation.13 | async-start | bytes 8388608
  350.9 18.5 %slice-start.1 = ((s8[12582912]{0:T(1024)(128)(4,1)}), s8[4194304]{0:T(1024)(128)(4,1)S(1)}, s32[]{:S(2)}) async-start(s8[12582912]{0:T(1024)(128)(4,1)} %bitcast.48), calls=%async_computation.14 | async-start | bytes 8388608
  359.9 9.5 slice-start.2
  378.6 1.2 copy-start.11
  378.6 2.2 copy-start.2
  378.7 2.2 copy-start.15
  379.9 0.9 copy-start.6
  385.0 457.5 %reduce-scatter.9.cloned.1.call-start = ((), (), s32[]{:S(2)}) async-start(), calls=%async_computation.10 | async-start | bytes 4866048 | tf_op jit(solution)/shard_map/reduce_scatter | solution.py:181
  392.4 1.1 copy-start.10
  392.4 683.8 %reduce-scatter.11.cloned.1.call-start = ((), (), s32[]{:S(2)}) async-start(), calls=%async_computation.11 | async-start | bytes 4866048 | tf_op jit(solution)/shard_map/reduce_scatter | solution.py:187
  402.2 4.5 copy-start.14
  402.2 5.1 copy-start.7
  402.2 899.4 %reduce-scatter.7.cloned.1.call-start = ((), (), s32[]{:S(2)}) async-start(), calls=%async_computation.9 | async-start | bytes 1216512 | tf_op jit(solution)/shard_map/reduce_scatter | solution.py:272
  405.3 936.5 %all-reduce.24.cloned.1.call-start = ((), (), s32[]{:S(2)}) async-start(), calls=%async_computation.12 | async-start | bytes 811008 | tf_op jit(solution)/shard_map/psum | solution.py:282
Sparse Core Ops, SparseCore 0:
  11.1 81.1 all-gather.4
  95.3 64.8 all-gather.6
  163.3 81.6 all-gather.8
  247.9 81.8 all-gather.10
  385.1 223.7 reduce-scatter.4
  614.7 227.7 reduce-scatter.8
  848.4 227.7 reduce-scatter.10
  1081.8 219.8 reduce-scatter.6
  1304.6 37.1 all-reduce.23
where the time goes:
time: 1360 us; the launch traced here: 1350 us
  waiting for transfers between devices  865 us (64%)
  blocking collectives  323 us (24%)
  matrix products  99.3 us (7%)
  other arithmetic  31.7 us (2%)
  between operations  17.7 us (1%)
  local copies, waits for them, and re-layouts  16.7 us (1%)
    unnamed x2, blocking collectives  309 us
    reduce_scatter x1, waiting for transfers between devices, shards(): lax.psum_scatter(mlp_local[4].astype(jnp.bfloat16), 'fsdp', scatter_dimen...  234 us
    reduce_scatter x1, waiting for transfers between devices, shards(): lax.psum_scatter(mlp_local[2].astype(jnp.bfloat16), 'fsdp', scatter_dimen...  234 us
    reduce_scatter x1, waiting for transfers between devices, shards(): lax.psum_scatter(attn_local[5].astype(jnp.bfloat16), 'fsdp', scatter_dime...  222 us
    all_gather x1, waiting for transfers between devices, shards(): lax.all_gather(mlp_shards[4], 'fsdp', axis=0, tiled=True)  76.6 us
    all_gather x1, waiting for transfers between devices, shards(): lax.all_gather(mlp_shards[2], 'fsdp', axis=0, tiled=True)  40.1 us
    reduce_scatter x1, waiting for transfers between devices, shards(): lax.psum_scatter(attn_local[2].astype(jnp.bfloat16), 'fsdp', scatter_dime...  35.1 us
  transfers between devices with their start and end apart: 9, of which 7 were waited for; matrix products, arithmetic and copies ran while one was open for 6% of the time, Pallas kernels for 0%

commit v1 on v0

v1 whole, which is shorter than its diff:
```python
import functools

import jax
import jax.numpy as jnp
from jax import lax
from jax.experimental import pallas as pl
from jax.experimental.pallas import tpu as pltpu
from jax.sharding import PartitionSpec as P

MESH = pl.DeviceIdType.MESH
BF = jnp.bfloat16
F32 = jnp.float32
EPSILON = 1e-06
ROWS, D, FF, HEADS, HEAD = 512, 768, 3072, 12, 64
TILE = 384
SMALL = 128
LOW = -1e30


def nn(left, right):
    return jnp.dot(left, right, preferred_element_type=F32)


def nt(left, right):
    return lax.dot_general(left, right, (((1,), (1,)), ((), ())), preferred_element_type=F32)


def tn(left, right):
    return lax.dot_general(left, right, (((0,), (0,)), ((), ())), preferred_element_type=F32)


class Where:
    def __init__(self):
        self.r = lax.axis_index("rep")
        self.f = lax.axis_index("fsdp")
        self.zl, self.core = self.r // 2, self.r % 2
        self.x, self.zh, self.y = self.f // 8, (self.f // 4) % 2, self.f % 4
        self.zo = 1 - self.zh
        c = self.core
        self.a = self.y + c * (self.x - self.y)
        self.b = self.x + c * (self.y - self.x)
        self.ap, self.a2, self.am = (self.a + 1) % 4, (self.a + 2) % 4, (self.a + 3) % 4
        self.bp, self.b2, self.bm = (self.b + 1) % 4, (self.b + 2) % 4, (self.b + 3) % 4
        self.a_up, self.a_down = self.at(1, 0), self.at(3, 0)
        self.b_up, self.b_down = self.at(0, 1), self.at(0, 3)
        self.twin = {"rep": self.r + 1 - 2 * c, "fsdp": self.f}
        other = (1 - self.zl) * 2 + c
        self.cross = {"rep": other, "fsdp": (self.x * 2 + self.zo) * 4 + self.y}
        self.pair = {"rep": other, "fsdp": self.f}

    def at(self, da, db):
        c = self.core
        y = (self.y + (1 - c) * da + c * db) % 4
        x = (self.x + c * da + (1 - c) * db) % 4
        return {"rep": self.r, "fsdp": (x * 2 + self.zh) * 4 + y}

    def greet(self):
        sem = pltpu.get_barrier_semaphore()
        for device in (self.a_up, self.a_down, self.b_up, self.b_down, self.twin, self.cross, self.pair):
            pl.semaphore_signal(sem, inc=1, device_id=device, device_id_type=MESH)

    def meet(self):
        pl.semaphore_wait(pltpu.get_barrier_semaphore(), 7)


class Copies:
    def remote(self, k, src, dst, device):
        return pltpu.make_async_remote_copy(
            src_ref=src,
            dst_ref=dst,
            send_sem=self.ss.at[k],
            recv_sem=self.rs.at[k],
            device_id=device,
            device_id_type=MESH,
        )

    def send(self, *which):
        for k in which:
            self.remote(k, *self.route(k)).start()

    def take(self, *which):
        for k in which:
            here = self.lands(k)
            self.remote(k, here, here, self.w.twin).wait_recv()

    def end(self):
        for k in range(self.count):
            self.remote(k, *self.route(k)).wait_send()


class Gather(Copies):
    count = 16

    def __init__(self, w, src, raw, ss, rs):
        self.w, self.src, self.raw, self.ss, self.rs = w, src, raw, ss, rs
        self.half = src.shape[1] // 2

    def own(self):
        return self.src.at[:, pl.ds(pl.multiple_of(self.w.core * self.half, 128), self.half)]

    def slot(self, *i):
        return self.raw.at[(self.w.core, *i)]

    def route(self, k):
        w = self.w
        if k < 3:
            return self.own(), self.slot(w.b, w.zh, w.a), (w.cross, w.a_up, w.a_down)[k]
        place, device = {
            3: ((w.b, w.zo, w.a), w.a_up),
            4: ((w.b, w.zo, w.a), w.a_down),
            5: ((w.b, 0, w.am), w.a_up),
            6: ((w.b, 1, w.ap), w.a_down),
            7: ((w.b,), w.b_up),
            8: ((w.b,), w.b_down),
            9: ((w.bm, 0), w.b_up),
            10: ((w.bp, 1), w.b_down),
            11: ((w.b,), w.twin),
            12: ((w.bm,), w.twin),
            13: ((w.bp,), w.twin),
            14: ((w.b2, 0), w.twin),
            15: ((w.b2, 1), w.twin),
        }[k]
        here = self.slot(*place)
        return here, here, device

    def lands(self, k):
        w = self.w
        if k >= 11:
            o = 1 - w.core
            return self.raw.at[
                {
                    11: (o, w.a),
                    12: (o, w.am),
                    13: (o, w.ap),
                    14: (o, w.a2, 0),
                    15: (o, w.a2, 1),
                }[k]
            ]
        return self.slot(
            *{
                0: (w.b, w.zo, w.a),
                1: (w.b, w.zh, w.am),
                2: (w.b, w.zh, w.ap),
                3: (w.b, w.zo, w.am),
                4: (w.b, w.zo, w.ap),
                5: (w.b, 0, w.a2),
                6: (w.b, 1, w.a2),
                7: (w.bm,),
                8: (w.bp,),
                9: (w.b2, 0),
                10: (w.b2, 1),
            }[k]
        )

    def g0(self):
        w = self.w
        self.send(0, 1, 2)
        self.raw[w.core, w.b, w.zh, w.a] = self.own()[...]

    def g1(self):
        self.take(0)
        self.send(3, 4)

    def g2(self):
        self.take(1, 2, 3, 4)
        self.send(5, 6)

    def g3(self):
        self.take(5, 6)
        self.send(7, 8, 11)

    def g4(self):
        self.take(7, 8)
        self.send(9, 10, 12, 13)

    def g5(self):
        self.take(9, 10)
        self.send(14, 15)

    def g6(self):
        self.take(11, 12, 13, 14, 15)


class Reduce(Copies):
    count = 19

    def __init__(self, w, part, columns, bufs, ss, rs):
        self.w, self.part, self.ss, self.rs = w, part, ss, rs
        self.tw, self.r1, self.fx, self.ar, self.af, self.zr, self.pr, self.done = bufs
        self.rows, self.columns = self.tw.shape[-2], pl.ds(columns, self.tw.shape[-1])

    def s(self, h, *i):
        left = (slice(None),) * (4 - 1 - len(i))
        return self.part.at[(h, *i, *left, slice(0, self.rows), self.columns)]

    def route(self, k):
        w, c = self.w, self.w.core
        if k < 4:
            j = (w.a2, w.ap, w.am, w.a)[k]
            return self.s(1 - c, j), self.tw.at[j], w.twin
        if k == 18:
            return self.done.at[c], self.done.at[c], w.twin
        place, device = {
            4: ((w.b2, 0), w.b_up),
            5: ((w.b2, 1), w.b_down),
            6: ((w.bp, 1), w.b_up),
            7: ((w.bm, 0), w.b_down),
            8: ((w.bp, 0), w.b_up),
            9: ((w.bm, 1), w.b_down),
            10: ((w.b, 0, w.a2), w.a_up),
            11: ((w.b, 1, w.a2), w.a_down),
            12: ((w.b, 1, w.ap), w.a_up),
            13: ((w.b, 0, w.am), w.a_down),
            14: ((w.b, 0, w.ap), w.a_up),
            15: ((w.b, 1, w.am), w.a_down),
            16: ((w.b, w.zo, w.a), w.cross),
            17: ((w.b, w.zh, w.a), w.pair),
        }[k]
        return self.s(c, *place), self.lands(k), device

    def lands(self, k):
        w = self.w
        if k < 4:
            return self.tw.at[(w.b2, w.bp, w.bm, w.b)[k]]
        if k == 18:
            return self.done.at[1 - w.core]
        return {
            4: self.r1.at[0],
            5: self.r1.at[1],
            6: self.fx.at[0, 1],
            7: self.fx.at[1, 0],
            8: self.fx.at[0, 0],
            9: self.fx.at[1, 1],
            10: self.ar.at[0],
            11: self.ar.at[1],
            12: self.af.at[0, 1],
            13: self.af.at[1, 0],
            14: self.af.at[0, 0],
            15: self.af.at[1, 1],
            16: self.zr,
            17: self.pr,
        }[k]

    def add(self, place, *terms):
        here = self.s(self.w.core, *place)
        total = here[...].astype(F32)
        for term in terms:
            total = total + term[...].astype(F32)
        here[...] = total.astype(BF)

    def add8(self, b, *terms):
        def one(i, _):
            z, a = i // 4, i % 4
            self.add((b, z, a), *[t.at[z, a] for t in terms])
            return 0

        lax.fori_loop(0, 8, one, 0)

    def add4(self, b, z, term):
        def one(a, _):
            self.add((b, z, a), term.at[a])
            return 0

        lax.fori_loop(0, 4, one, 0)

    def r0(self):
        self.send(0, 1, 2, 3)

    def r1_(self):
        w = self.w
        self.take(0)
        self.add8(w.b2, self.tw.at[w.b2])
        self.send(4, 5)
        self.take(1)
        self.add8(w.bp, self.tw.at[w.bp])
        self.send(6)
        self.take(2)
        self.add8(w.bm, self.tw.at[w.bm])
        self.send(7)

    def r2(self):
        w = self.w
        self.take(3)
        self.add8(w.b, self.tw.at[w.b])
        self.take(4)
        self.add4(w.bp, 0, self.r1.at[0])
        self.send(8)
        self.take(5)
        self.add4(w.bm, 1, self.r1.at[1])
        self.send(9)

    def r3(self):
        self.take(6, 7, 8, 9)
        self.add8(self.w.b, self.fx.at[0], self.fx.at[1])
        self.send(10, 11, 12, 13)

    def r4(self):
        w = self.w
        self.take(10, 11)
        self.add((w.b, 0, w.ap), self.ar.at[0])
        self.send(14)
        self.add((w.b, 1, w.am), self.ar.at[1])
        self.send(15)

    def r5(self):
        w = self.w
        self.take(12, 13, 14, 15)
        for z in range(2):
            self.add((w.b, z, w.a), self.af.at[0, z], self.af.at[1, z])
        self.send(16)

    def r6(self):
        w = self.w
        self.take(16)
        self.add((w.b, w.zh, w.a), self.zr)
        self.send(17)

    def r7(self):
        w = self.w
        self.take(17)
        self.done[w.core] = self.s(w.core, w.b, w.zh, w.a)[...].astype(F32) + self.pr[...].astype(F32)
        self.send(18)

    def r8(self):
        self.take(18)


STAGES = ("r0", "r1_", "r2", "r3", "r4", "r5", "r6", "r7", "r8")


def reduce_scratch(rows, half):
    return [
        pltpu.VMEM((4, 2, 4, rows, half), BF),
        pltpu.VMEM((2, 4, rows, half), BF),
        pltpu.VMEM((2, 2, 4, rows, half), BF),
        pltpu.VMEM((2, rows, half), BF),
        pltpu.VMEM((2, 2, rows, half), BF),
        pltpu.VMEM((rows, half), BF),
        pltpu.VMEM((rows, half), BF),
        pltpu.VMEM((2, rows, half), F32),
    ]


def assemble(raw, out, width):
    rows = raw.shape[4]

    def one(g, _):
        x, z = g // 2, g % 2
        place = pl.ds(pl.multiple_of(g * 4 * rows, 4 * rows), 4 * rows)
        for h in range(2):
            parts = [
                raw[0, x, z, y, :, :width] if h == 0 else raw[1, y, z, x, :, :width] for y in range(4)
            ]
            out[place, h * width : (h + 1) * width] = jnp.concatenate(parts, axis=0)
        return 0

    lax.fori_loop(0, 8, one, 0)


def scatter_rows(value, part, h, first):
    n = value.shape[1]
    for f in range(32):
        x, z, y = f // 8, (f // 4) % 2, f % 4
        part[h, x + h * (y - x), z, y + h * (x - y), :, pl.ds(first, n)] = value[
            24 * f : 24 * f + 24
        ].astype(BF)


def stats(x):
    centred = x - jnp.mean(x, axis=1, keepdims=True)
    inv = lax.rsqrt(jnp.mean(centred * centred, axis=1, keepdims=True) + EPSILON)
    return centred * inv, inv


def norm_backward(grad, normed, inv, gain):
    e = grad * gain
    return inv * (
        e - jnp.mean(e, axis=1, keepdims=True) - normed * jnp.mean(e * normed, axis=1, keepdims=True)
    )


def column_sum(v):
    return jnp.sum(v, axis=0, keepdims=True)


def iota(shape, d):
    return lax.broadcasted_iota(jnp.int32, shape, d)


def by24(n):
    return lax.shift_right_logical(n * 2731, 16)


def select24():
    n = iota((SMALL, D), 1)
    return (n - 24 * by24(n) == iota((SMALL, D), 0)).astype(F32).astype(BF)


def select96():
    n = iota((SMALL, FF), 1)
    return (n - 96 * lax.shift_right_logical(by24(n), 2) == iota((SMALL, FF), 0)).astype(F32).astype(BF)


def row_blocks(count, body):
    step = ROWS // count

    def one(i, c):
        return body(pl.ds(pl.multiple_of(i * step, step), step), c)

    return one


def kernel(
    tokens, lengths, pads, og, in_shard, out_shard, up_shard, down_shard,
    layer_out, input_grad, d_in, d_out, d_up, d_down, d_small,
    raw_in, raw_out, raw_up, raw_down, small, w_in, w_out, w_up, w_down,
    h1, joint, lse, attended, residual, h2, h2t, dh2, vec, ub, gvec, dub,
    gs, gr, rs, rr, *bufs,
):
    w = Where()
    w.greet()
    gq, go, gu, gd = [
        Gather(w, s, r, gs.at[i], gr.at[i])
        for i, (s, r) in enumerate(
            ((in_shard, raw_in), (out_shard, raw_out), (up_shard, raw_up), (down_shard, raw_down))
        )
    ]
    every = (gq, go, gu, gd)
    places = [(raw_up, 0), (raw_up, 768), (raw_down, 0), (raw_out, 0)]
    places += [(raw_in, 0), (raw_in, 384), (raw_in, 768), (small, 0)]
    ru0, ru1, rd, ro, rq0, rq1, rq2, rv = [
        Reduce(w, part, first, bufs[8 * i : 8 * i + 8], rs.at[i], rr.at[i])
        for i, (part, first) in enumerate(places)
    ]

    gvec[...] = jnp.zeros_like(gvec)

    def codes(dim):
        pos = iota((ROWS, 1) if dim == 0 else (1, ROWS), dim)
        seg = jnp.zeros_like(pos)
        start = jnp.int32(0)
        for j in range(lengths.shape[1]):
            seg = seg + (pos >= start).astype(jnp.int32)
            start = start + lengths[0, j]
        return jnp.where(pos < ROWS - pads[0, 0], seg, -1 - pos)

    w.meet()
    for g in every:
        g.g0()
    for g in every:
        g.g1()
    for g in every:
        g.g2()
    for g in every:
        g.g3()
    gq.g4()
    gq.g5()
    go.g4()
    gu.g4()
    gd.g4()
    gq.g6()
    assemble(raw_in, w_in, 1152)

    packed = raw_in[0, :, :, :, 0:16, 1152:1280].reshape(32 * 16, SMALL)
    spread = nn(packed, select24())
    n, row = iota((ROWS, D), 1), iota((ROWS, D), 0)
    spread = jnp.where(by24(n) == lax.shift_right_logical(row, 4), spread, 0.0)
    vec[...] = jnp.sum(spread.reshape(32, 16, D), axis=0)
    packed = raw_in[0, :, :, :, 0:16, 1152:1280].reshape(32, 16, SMALL)[:, 8:9].reshape(32, SMALL)
    spread = nn(packed, select96())
    n, row = iota((32, FF), 1), iota((32, FF), 0)
    ub[...] = column_sum(jnp.where(lax.shift_right_logical(by24(n), 2) == row, spread, 0.0))

    def norm_one(rows, c):
        normed, _ = stats(tokens[rows, :].astype(F32))
        h1[rows, :] = (normed * vec[0:1, :] + vec[1:2, :]).astype(BF)
        return c

    lax.fori_loop(0, 4, row_blocks(4, norm_one), 0)

    for t in range(3):
        bias = (vec[2:3, :], jnp.zeros((1, D), F32), vec[3:4, :])[t]
        for u in range(2):
            columns = slice(t * D + u * TILE, t * D + (u + 1) * TILE)
            joint[:, columns] = (nn(h1[...], w_in[:, columns]) + bias[:, u * TILE : (u + 1) * TILE]).astype(BF)

    same = codes(0)
    lane = iota((1, 128), 1)

    def scores(queries, keys, first):
        mine = (lane >= 64 * first) & (lane < 64 * first + 64)
        picked = jnp.where(mine, queries.astype(F32) * HEAD**-0.5, 0.0).astype(BF)
        return jnp.where(same == codes(1), nt(keys, picked), LOW)

    def pair_columns(p):
        return [pl.ds(pl.multiple_of(t * D + p * 128, 128), 128) for t in range(3)]

    def attend(p, c):
        cq, ck, cv = pair_columns(p)
        queries, keys, values = joint[:, cq], joint[:, ck], joint[:, cv]
        mixed = None
        for first in range(2):
            s = scores(queries, keys, first)
            top = jnp.max(s, axis=0, keepdims=True)
            e = jnp.exp(s - top)
            total = jnp.sum(e, axis=0, keepdims=True)
            weights = (e * (1.0 / total)).astype(BF)
            lse[2 * p + first] = top + jnp.log(total)
            o = tn(weights, values)
            mixed = o if first == 0 else jnp.where(lane < 64, mixed, o)
        attended[:, cq] = mixed.astype(BF)

        @pl.when(p == 0)
        def _():
            go.g5()

        @pl.when(p == 1)
        def _():
            gu.g5()

        @pl.when(p == 3)
        def _():
            gd.g5()

        return c

    lax.fori_loop(0, 6, attend, 0)

    go.g6()
    assemble(raw_out, w_out, TILE)
    for u in range(2):
        columns = slice(u * TILE, (u + 1) * TILE)
        residual[:, columns] = (
            tokens[:, columns].astype(F32) + nn(attended[...], w_out[:, columns]) + vec[4:5, columns]
        )

    def norm_two(rows, c):
        normed, _ = stats(residual[rows, :])
        h2[rows, :] = (normed * vec[5:6, :] + vec[6:7, :]).astype(BF)
        return c

    lax.fori_loop(0, 4, row_blocks(4, norm_two), 0)
    h2t[...] = h2[...].T
    gu.g6()
    assemble(raw_up, w_up, 1536)
    gd.g6()
    assemble(raw_down, w_down, TILE)
    for g in every:
        g.end()

    input_grad[...] = residual[...] + vec[7:8, :]
    dh2[...] = jnp.zeros_like(dh2)

    def tile(i, c):
        t = i // 2 + 4 * (i % 2)
        columns = pl.ds(pl.multiple_of(t * TILE, TILE), TILE)
        u = nn(h2[...], w_up[:, columns]) + ub[:, columns]
        k = 0.7978845608028654
        th = jnp.tanh(k * (u + 0.044715 * (u * u * u)))
        low = 0.5 * (1.0 + th)
        act = (u * low).astype(BF)
        slope = low + (0.5 * k) * u * (1.0 - th * th) * (1.0 + (3 * 0.044715) * (u * u))
        down = w_down[columns, :]
        input_grad[...] += nn(act, down)
        grad_pre = (nt(og[...], down) * slope).astype(BF)
        dub[:, columns] = column_sum(grad_pre.astype(F32))
        scatter_rows(nn(h2t[...], grad_pre), raw_up, t // 4, pl.multiple_of((t % 4) * TILE, 128))
        dh2[...] += nt(grad_pre, w_up[:, columns])
        grad_down = tn(act, og[...]).astype(BF)
        x, z = t // 2, t % 2
        for y in range(4):
            raw_down[0, x, z, y] = grad_down[96 * y : 96 * y + 96, :TILE]
            raw_down[1, y, z, x] = grad_down[96 * y : 96 * y + 96, TILE:]

        @pl.when(i == 3)
        def _():
            ru0.r0()

        @pl.when(i == 4)
        def _():
            ru0.r1_()

        @pl.when(i == 5)
        def _():
            ru0.r2()

        return c

    lax.fori_loop(0, 8, tile, 0)
    rd.r0()
    ru1.r0()
    ru0.r3()
    layer_out[...] = input_grad[...].astype(BF)

    def back_two(rows, c):
        normed, inv = stats(residual[rows, :])
        grad = dh2[rows, :]
        up = og[rows, :].astype(F32)
        total = up + norm_backward(grad, normed, inv, vec[5:6, :])
        residual[rows, :] = total
        rounded = total.astype(BF)
        w_up[rows, 0:D] = rounded
        return (
            c[0] + column_sum(rounded.astype(F32)),
            c[1] + column_sum(grad * normed),
            c[2] + column_sum(grad),
            c[3] + column_sum(up),
        )

    zero = jnp.zeros((1, D), F32)
    sums = lax.fori_loop(0, 4, row_blocks(4, back_two), (zero, zero, zero, zero))
    for j, v in zip((4, 5, 6, 7), sums):
        gvec[j : j + 1, :] = v
    rd.r1_()
    grad_branch = w_up.at[0:ROWS, 0:D]
    grad_attended = w_up.at[0:ROWS, D : 2 * D]
    for u in range(2):
        columns = slice(u * TILE, (u + 1) * TILE)
        scatter_rows(tn(attended[...], grad_branch[:, columns]), raw_out, u, 0)
        grad_attended[:, columns] = nt(grad_branch[...], w_out[columns, :]).astype(BF)
    ro.r0()
    ru1.r1_()
    rd.r2()
    ru0.r4()
    h1t = h2t
    h1t[...] = h1[...].T

    def attend_back(p, c):
        cq, ck, cv = pair_columns(p)
        queries, keys, values = joint[:, cq], joint[:, ck], joint[:, cv]
        gradient = grad_attended[:, cq]
        dq = dk = dv = None
        for first in range(2):
            mine = (lane >= 64 * first) & (lane < 64 * first + 64)
            weights = jnp.exp(scores(queries, keys, first) - lse[2 * p + first])
            picked = jnp.where(mine, gradient, jnp.zeros_like(gradient))
            grad_weights = nt(values, picked)
            along = jnp.sum(grad_weights * weights, axis=0, keepdims=True)
            grad_scores = (weights * (grad_weights - along)).astype(BF)
            v = nn(weights.astype(BF), gradient)
            k = nn(grad_scores, queries) * HEAD**-0.5
            q = tn(grad_scores, keys) * HEAD**-0.5
            if first == 0:
                dq, dk, dv = q, k, v
            else:
                dq, dk, dv = [jnp.where(lane < 64, l, r) for l, r in ((dq, q), (dk, k), (dv, v))]
        dq, dk, dv = dq.astype(BF), dk.astype(BF), dv.astype(BF)
        joint[:, cq], joint[:, ck], joint[:, cv] = dq, dk, dv
        gvec[2:3, cq] = column_sum(dq.astype(F32))
        gvec[3:4, cq] = column_sum(dv.astype(F32))
        both = jnp.concatenate([dq, dk, dv], axis=1)
        scatter_rows(nn(h1t[...], both), raw_in, p % 2, pl.multiple_of((p // 2) * TILE, 128))
        plan = (
            (ro.r1_, ru1.r2, rd.r3, ru0.r5),
            (rq0.r0, ro.r2, ru1.r3, rd.r4, ru0.r6),
            (rq0.r1_, ro.r3, ru1.r4, rd.r5, ru0.r7),
            (rq1.r0, rq0.r2, ro.r4, ru1.r5, rd.r6, ru0.r8),
            (rq1.r1_, rq0.r3, ro.r5, ru1.r6, rd.r7),
            (rq2.r0, rq1.r2, rq0.r4, ro.r6, ru1.r7, rd.r8),
        )
        for i, stages in enumerate(plan):

            @pl.when(p == i)
            def _(stages=stages):
                for stage in stages:
                    stage()

        return c

    lax.fori_loop(0, 6, attend_back, 0)

    rq2.r1_()
    for u in range(2):
        columns = slice(u * TILE, (u + 1) * TILE)
        dh2[:, columns] = nt(joint[...], w_in[columns, :])
    rq2.r2()
    rq1.r3()
    rq0.r5()
    ro.r7()
    ru1.r8()

    def back_one(rows, c):
        normed, inv = stats(tokens[rows, :].astype(F32))
        grad = dh2[rows, :]
        input_grad[rows, :] = residual[rows, :] + norm_backward(grad, normed, inv, vec[0:1, :])
        return c[0] + column_sum(grad * normed), c[1] + column_sum(grad)

    sums = lax.fori_loop(0, 4, row_blocks(4, back_one), (zero, zero))
    for j, v in zip((0, 1), sums):
        gvec[j : j + 1, :] = v

    n, row = iota((32, 16, D), 2), iota((32, 16, D), 0)
    spread = jnp.where(by24(n) == row, jnp.broadcast_to(gvec[...][None], (32, 16, D)), 0.0)
    own = nt(spread.reshape(512, D).astype(BF), select24()).astype(BF).reshape(32, 16, SMALL)
    n, row = iota((32, FF), 1), iota((32, FF), 0)
    spread = jnp.where(lax.shift_right_logical(by24(n), 2) == row, jnp.broadcast_to(dub[...], (32, FF)), 0.0)
    hidden = nt(spread.astype(BF), select96())
    for f in range(32):
        x, z, y = f // 8, (f // 4) % 2, f % 4
        small[0, x, z, y] = own[f]
        small[1, y, z, x] = jnp.broadcast_to(hidden[f : f + 1], (16, SMALL)).astype(BF)
    rv.r0()
    rq2.r3()
    rq1.r4()
    rv.r1_()
    rq0.r6()
    ro.r8()
    rv.r2()
    rq2.r4()
    rq1.r5()
    rv.r3()
    rq0.r7()
    rq2.r5()
    rv.r4()
    rq1.r6()
    rq0.r8()
    rq2.r6()
    rv.r5()
    rq1.r7()
    rv.r6()
    rq2.r7()
    rq1.r8()
    rv.r7()
    rq2.r8()
    rv.r8()

    for h in range(2):
        d_up[:, h * 1536 : h * 1536 + 768] = ru0.done[h]
        d_up[:, h * 1536 + 768 : h * 1536 + 1536] = ru1.done[h]
        d_down[:, h * TILE : (h + 1) * TILE] = rd.done[h]
        d_out[:, h * TILE : (h + 1) * TILE] = ro.done[h]
        d_small[h] = rv.done[h]
        for k, r in enumerate((rq0, rq1, rq2)):
            for j in range(3):
                to = j * D + (2 * k + h) * 128
                d_in[:, to : to + 128] = r.done[h, :, 128 * j : 128 * j + 128]
    for r in (ru0, ru1, rd, ro, rq0, rq1, rq2, rv):
        r.end()


def shards(
    tokens, image_lengths, pad_counts, out_grad, first_gain, first_shift, input_weight, query_bias,
    value_bias, output_weight, output_bias, second_gain, second_shift, up_weight, up_bias, down_weight,
    down_bias,
):
    vectors = jnp.stack(
        [first_gain, first_shift, query_bias, value_bias, output_bias, second_gain, second_shift, down_bias]
    )
    vectors = jnp.pad(vectors, ((0, 0), (0, SMALL - 24)))
    hidden = jnp.pad(up_bias[None], ((0, 15), (0, SMALL - 96)))
    packed = jnp.concatenate([vectors, hidden], axis=0)
    in_shard = jnp.concatenate(
        [input_weight[:, :1152], packed, input_weight[:, 1152:], jnp.zeros((24, SMALL), BF)], axis=1
    )
    vmem = pl.BlockSpec(memory_space=pltpu.VMEM)
    smem = pl.BlockSpec(memory_space=pltpu.SMEM)
    scratch = [
        pltpu.VMEM((2, 4, 2, 4, 24, 1280), BF),
        pltpu.VMEM((2, 4, 2, 4, 24, 384), BF),
        pltpu.VMEM((2, 4, 2, 4, 24, 1536), BF),
        pltpu.VMEM((2, 4, 2, 4, 96, 384), BF),
        pltpu.VMEM((2, 4, 2, 4, 16, SMALL), BF),
        pltpu.VMEM((D, 3 * D), BF),
        pltpu.VMEM((D, D), BF),
        pltpu.VMEM((D, FF), BF),
        pltpu.VMEM((FF, D), BF),
        pltpu.VMEM((ROWS, D), BF),
        pltpu.VMEM((ROWS, 3 * D), BF),
        pltpu.VMEM((HEADS, 1, ROWS), F32),
        pltpu.VMEM((ROWS, D), BF),
        pltpu.VMEM((ROWS, D), F32),
        pltpu.VMEM((ROWS, D), BF),
        pltpu.VMEM((D, ROWS), BF),
        pltpu.VMEM((ROWS, D), F32),
        pltpu.VMEM((16, D), F32),
        pltpu.VMEM((1, FF), F32),
        pltpu.VMEM((16, D), F32),
        pltpu.VMEM((1, FF), F32),
        pltpu.SemaphoreType.DMA((4, 16)),
        pltpu.SemaphoreType.DMA((4, 16)),
        pltpu.SemaphoreType.DMA((8, 19)),
        pltpu.SemaphoreType.DMA((8, 19)),
    ]
    for rows, half in ((24, 768), (24, 768), (96, 384), (24, 384), (24, 384), (24, 384), (24, 384), (16, SMALL)):
        scratch += reduce_scratch(rows, half)
    shape = jax.ShapeDtypeStruct
    layer_out, input_grad, d_in, d_out, d_up, d_down, d_small = pl.pallas_call(
        kernel,
        out_shape=[
            shape((ROWS, D), BF),
            shape((ROWS, D), F32),
            shape((24, 3 * D), F32),
            shape((24, D), F32),
            shape((24, FF), F32),
            shape((96, D), F32),
            shape((2, 16, SMALL), F32),
        ],
        in_specs=[vmem, smem, smem, vmem, vmem, vmem, vmem, vmem],
        out_specs=[vmem] * 7,
        scratch_shapes=scratch,
        compiler_params=pltpu.CompilerParams(
            collective_id=0, has_side_effects=True, vmem_limit_bytes=63 << 20
        ),
        cost_estimate=pl.CostEstimate(flops=25 * 10**9, bytes_accessed=6 * 10**6, transcendentals=8 * 10**6),
    )(
        tokens, image_lengths, pad_counts.reshape(1, 1), out_grad, in_shard, output_weight, up_weight, down_weight
    )
    v = [d_small[0, j, :24] for j in range(8)]
    return (
        layer_out, input_grad, v[0], v[1], d_in, v[2], v[3], d_out, v[4], v[5], v[6], d_up,
        d_small[1, 0, :96], d_down, v[7],
    )


def solution(mesh):
    tall, flat, part = P(("rep", "fsdp"), None), P("fsdp"), P("fsdp", None)
    return jax.shard_map(
        shards,
        mesh=mesh,
        in_specs=(
            tall, tall, P(("rep", "fsdp")), tall, flat, flat, part, flat, flat, part, flat, flat, flat,
            part, flat, part, flat,
        ),
        out_specs=(
            tall, tall, flat, flat, part, flat, flat, part, flat, flat, flat, part, flat, part, flat,
        ),
        check_vma=False,
    )
```

time: 1360 us -> 172 us (0.13)
  waiting for transfers between devices: 865 us -> 0 us
  blocking collectives: 323 us -> 0 us
  Pallas kernels: 0 us -> 159 us
  matrix products: 99.3 us -> 0 us
  other arithmetic: 31.7 us -> 1.33 us
  between operations: 17.7 us -> 1.34 us
    reduce_scatter x4 -> x0, waiting for transfers between devices: 724 us -> none  [the longest x1 234 us: shards(): lax.psum_scatter(mlp_local[4].astype(jnp.bfloat16), 'fsdp', scatter_dimen...]
    unnamed x2 -> x0, blocking collectives: 309 us -> none
    pallas_call x0 -> x1, Pallas kernels: none -> 159 us  [shards(): pl.pallas_call(kernel, out_shape=[shape((ROWS, D), BF), shape((ROWS, D),...]
    all_gather x4 -> x0, waiting for transfers between devices: 117 us -> none  [the longest x1 76.6 us: shards(): lax.all_gather(mlp_shards[4], 'fsdp', axis=0, tiled=True)]
    dot_general x18 -> x0, matrix products: 99.3 us -> none  [the longest x4 23.1 us: transposed(): lax.dot_general(left, right, (((0,), (0,)), ((), ())), preferred_element_...]
    psum x1 -> x0, waiting for transfers between devices: 21.4 us -> none  [shards(): lax.psum(attn_part[2].astype(jnp.bfloat16), 'rep').astype(jnp.float32)]
    convert_element_type x22 -> x0, other arithmetic: 17.3 us -> none  [the longest x1 7.16 us: shards(): grad_scores = (weights * (grad_weights - jnp.sum(grad_weights * weights,...]
  transfers between devices with their start and end apart: 9 -> 0, of which waited for: 7 -> 0; matrix products, arithmetic and copies ran while one was open for 6% -> 0% of each run, Pallas kernels for 0% -> 0%
where the time goes in v1:
time: 172 us
  Pallas kernels  159 us (92%)
  local copies, waits for them, and re-layouts  10.5 us (6%)
    pallas_call x1, Pallas kernels, shards(): pl.pallas_call(kernel, out_shape=[shape((ROWS, D), BF), shape((ROWS, D),...  159 us
    unnamed x16, local copies, waits for them, and re-layouts  5.97 us

profile of v1, /device:TPU:1, one launch (start us, length us, event | category | flops | bytes accessed | tf_op | source)
XLA Modules:
  0.0 172.0 jit_solution(13184334335820345608)
XLA Ops:
  1.3 0.8 stack.35
  2.1 0.9 fusion.12
  3.0 1.3 fusion.11.in_shard
  4.3 158.9 %shard_map.280 = (bf16[512,768]{1,0:T(8,128)(2,1)}, f32[512,768]{1,0:T(8,128)}, f32[24,2304]{1,0:T(8,128)}, f32[24,768]{1,0:T(8,128)}, f32[24,3072]{1,0:T(8,128)...) custom-call(bf16[512,768]{1,0:T(8,128)(2,1)} %tokens.1, s32[1,6]{1,0:T(1,128)} %lengths.1, s32[1,1]{1,0:T(1,128)} %bitcast.28.pads, ...), custom_call_target="tpu_custom_call" | custom-call | flops 24999999488 | bytes 6000000 | tf_op jit(solution)/shard_map/pallas_call | solution.py:787
  163.2 0.0 copy-start
  163.2 1.3 slice_bitcast_fusion.1
  164.5 1.5 slice_bitcast_fusion
  166.0 2.1 %copy.39 = bf16[512,768]{1,0:T(8,128)(2,1)} copy(bf16[512,768]{1,0:T(8,128)(2,1)} %get-tuple-element.54) | data formatting | bytes 1572864
  168.1 0.0 copy-done
  168.1 0.0 copy-start.3
  168.1 0.0 copy-start.4
  168.1 0.0 copy-start.2
  168.1 0.0 copy-start.1
  168.1 1.1 copy.40
  169.2 0.0 copy-done.3
  169.2 0.7 copy.41
  169.9 0.0 copy-done.4
  169.9 0.6 copy.42
  170.6 0.0 copy-done.2
  170.6 0.7 copy.43
  171.3 0.0 copy-done.1
  171.3 0.7 copy.44
  (2 shorter events, 0.0 us)
Async XLA Ops:
  163.2 4.9 %copy-start = (f32[512,768]{1,0:T(8,128)S(1)}, f32[512,768]{1,0:T(8,128)}, u32[]{:S(2)}) copy-start(f32[512,768]{1,0:T(8,128)} %get-tuple-element.55) | copy-start | bytes 4718596
  168.1 1.2 copy-start.3
  168.1 1.9 %copy-start.4 = (f32[24,768]{1,0:T(8,128)S(1)}, f32[24,768]{1,0:T(8,128)}, u32[]{:S(2)}) copy-start(f32[24,768]{1,0:T(8,128)} %get-tuple-element.61) | copy-start | bytes 221188
  168.1 2.5 %copy-start.2 = (f32[24,3072]{1,0:T(8,128)S(1)}, f32[24,3072]{1,0:T(8,128)}, u32[]{:S(2)}) copy-start(f32[24,3072]{1,0:T(8,128)} %get-tuple-element.65) | copy-start | bytes 884740
  168.1 3.2 %copy-start.1 = (f32[96,768]{1,0:T(8,128)S(1)}, f32[96,768]{1,0:T(8,128)}, u32[]{:S(2)}) copy-start(f32[96,768]{1,0:T(8,128)} %get-tuple-element.67) | copy-start | bytes 884740

commit v2 on v1

--- a/solution.py
+++ b/solution.py
@@ -41,12 +41,13 @@
         self.b = self.x + c * (self.y - self.x)
         self.ap, self.a2, self.am = (self.a + 1) % 4, (self.a + 2) % 4, (self.a + 3) % 4
         self.bp, self.b2, self.bm = (self.b + 1) % 4, (self.b + 2) % 4, (self.b + 3) % 4
-        self.a_up, self.a_down = self.at(1, 0), self.at(3, 0)
-        self.b_up, self.b_down = self.at(0, 1), self.at(0, 3)
+        self.a_up, self.a_down, self.a_far = self.at(1, 0), self.at(3, 0), self.at(2, 0)
+        self.b_up, self.b_down, self.b_far = self.at(0, 1), self.at(0, 3), self.at(0, 2)
+        self.z = self.zh * 2 + self.zl
         self.twin = {"rep": self.r + 1 - 2 * c, "fsdp": self.f}
-        other = (1 - self.zl) * 2 + c
-        self.cross = {"rep": other, "fsdp": (self.x * 2 + self.zo) * 4 + self.y}
-        self.pair = {"rep": other, "fsdp": self.f}
+        self.pair = {"rep": (1 - self.zl) * 2 + c, "fsdp": self.f}
+        self.cross, self.cross_up, self.cross_down, self.cross_far = [self.over(i) for i in (0, 1, 3, 2)]
+        self.third = {"rep": self.r, "fsdp": (self.x * 2 + self.zo) * 4 + self.y}
 
     def at(self, da, db):
         c = self.core
@@ -54,13 +55,23 @@
         x = (self.x + c * da + (1 - c) * db) % 4
         return {"rep": self.r, "fsdp": (x * 2 + self.zh) * 4 + y}
 
+    def over(self, da):
+        c = self.core
+        y = (self.y + (1 - c) * da) % 4
+        x = (self.x + c * da) % 4
+        return {"rep": (1 - self.zl) * 2 + c, "fsdp": (x * 2 + self.zo) * 4 + y}
+
+    def friends(self):
+        near = [self.a_up, self.a_down, self.a_far, self.b_up, self.b_down, self.b_far, self.twin]
+        return near + [self.pair, self.third, self.cross, self.cross_up, self.cross_down, self.cross_far]
+
     def greet(self):
         sem = pltpu.get_barrier_semaphore()
-        for device in (self.a_up, self.a_down, self.b_up, self.b_down, self.twin, self.cross, self.pair):
+        for device in self.friends():
             pl.semaphore_signal(sem, inc=1, device_id=device, device_id_type=MESH)
 
     def meet(self):
-        pl.semaphore_wait(pltpu.get_barrier_semaphore(), 7)
+        pl.semaphore_wait(pltpu.get_barrier_semaphore(), len(self.friends()))
 
 
 class Copies:
@@ -91,9 +102,10 @@
 class Gather(Copies):
     count = 16
 
-    def __init__(self, w, src, raw, ss, rs):
-        self.w, self.src, self.raw, self.ss, self.rs = w, src, raw, ss, rs
+    def __init__(self, w, src, raw, direct, local, ss, rs):
+        self.w, self.src, self.raw, self.direct, self.ss, self.rs = w, src, raw, direct, ss, rs
         self.half = src.shape[1] // 2
+        self.local = pltpu.make_async_copy(self.own(), self.slot(w.b, w.zh, w.a), local)
 
     def own(self):
         return self.src.at[:, pl.ds(pl.multiple_of(self.w.core * self.half, 128), self.half)]
@@ -103,12 +115,14 @@
 
     def route(self, k):
         w = self.w
-        if k < 3:
-            return self.own(), self.slot(w.b, w.zh, w.a), (w.cross, w.a_up, w.a_down)[k]
+        own = (w.b, w.zh, w.a)
+        if k in (0, 1, 3) or (self.direct and k < 7):
+            to = (w.a_up, w.a_down, w.a_far, w.cross, w.cross_up, w.cross_down, w.cross_far)[k]
+            return self.own(), self.slot(*own), to
         place, device = {
-            3: ((w.b, w.zo, w.a), w.a_up),
-            4: ((w.b, w.zo, w.a), w.a_down),
-            5: ((w.b, 0, w.am), w.a_up),
+            2: ((w.b, 0, w.am), w.a_up),
+            4: ((w.b, w.zo, w.a), w.a_up),
+            5: ((w.b, w.zo, w.a), w.a_down),
             6: ((w.b, 1, w.ap), w.a_down),
             7: ((w.b,), w.b_up),
             8: ((w.b,), w.b_down),
@@ -125,6 +139,10 @@
 
     def lands(self, k):
         w = self.w
+        if not self.direct and k in (2, 6):
+            return self.slot(w.b, k // 6, w.a2)
+        if k < 7:
+            return self.slot(w.b, w.zh if k < 3 else w.zo, (w.am, w.ap, w.a2, w.a, w.am, w.ap, w.a2)[k])
         if k >= 11:
             o = 1 - w.core
             return self.raw.at[
@@ -136,58 +154,47 @@
                     15: (o, w.a2, 1),
                 }[k]
             ]
-        return self.slot(
-            *{
-                0: (w.b, w.zo, w.a),
-                1: (w.b, w.zh, w.am),
-                2: (w.b, w.zh, w.ap),
-                3: (w.b, w.zo, w.am),
-                4: (w.b, w.zo, w.ap),
-                5: (w.b, 0, w.a2),
-                6: (w.b, 1, w.a2),
-                7: (w.bm,),
-                8: (w.bp,),
-                9: (w.b2, 0),
-                10: (w.b2, 1),
-            }[k]
-        )
+        return self.slot(*{7: (w.bm,), 8: (w.bp,), 9: (w.b2, 0), 10: (w.b2, 1)}[k])
 
     def g0(self):
-        w = self.w
-        self.send(0, 1, 2)
-        self.raw[w.core, w.b, w.zh, w.a] = self.own()[...]
+        self.send(*((6, 4, 5, 2, 3, 0, 1) if self.direct else (3, 0, 1)))
+        self.local.start()
+
+    def g0a(self):
+        self.take(3)
+        self.send(4, 5)
+
+    def g0b(self):
+        self.take(0, 1, 4, 5)
+        self.send(2, 6)
 
     def g1(self):
-        self.take(0)
-        self.send(3, 4)
+        self.local.wait()
+        self.take(*((0, 1, 2, 3, 4, 5, 6) if self.direct else (2, 6)))
+        self.send(7, 8, 11)
 
     def g2(self):
-        self.take(1, 2, 3, 4)
-        self.send(5, 6)
-
-    def g3(self):
-        self.take(5, 6)
-        self.send(7, 8, 11)
-
-    def g4(self):
         self.take(7, 8)
         self.send(9, 10, 12, 13)
 
-    def g5(self):
+    def g3(self):
         self.take(9, 10)
         self.send(14, 15)
 
-    def g6(self):
+    def g4(self):
         self.take(11, 12, 13, 14, 15)
 
 
 class Reduce(Copies):
-    count = 19
-
-    def __init__(self, w, part, columns, bufs, ss, rs):
-        self.w, self.part, self.ss, self.rs = w, part, ss, rs
-        self.tw, self.r1, self.fx, self.ar, self.af, self.zr, self.pr, self.done = bufs
+    def __init__(self, w, part, columns, direct, bufs, ss, rs):
+        self.w, self.part, self.direct, self.ss, self.rs = w, part, direct, ss, rs
+        self.tw, self.fx, self.af, self.zb, self.done = bufs
         self.rows, self.columns = self.tw.shape[-2], pl.ds(columns, self.tw.shape[-1])
+        self.used = [k for k in range(17) if k not in ((7, 8, 9) if direct else ())]
+
+    def end(self):
+        for k in self.used:
+            self.remote(k, *self.route(k)).wait_send()
 
     def s(self, h, *i):
         left = (slice(None),) * (4 - 1 - len(i))
@@ -195,50 +202,55 @@
 
     def route(self, k):
         w, c = self.w, self.w.core
+        every = slice(None)
         if k < 4:
             j = (w.a2, w.ap, w.am, w.a)[k]
             return self.s(1 - c, j), self.tw.at[j], w.twin
-        if k == 18:
+        if k == 16:
             return self.done.at[c], self.done.at[c], w.twin
-        place, device = {
-            4: ((w.b2, 0), w.b_up),
-            5: ((w.b2, 1), w.b_down),
-            6: ((w.bp, 1), w.b_up),
-            7: ((w.bm, 0), w.b_down),
-            8: ((w.bp, 0), w.b_up),
-            9: ((w.bm, 1), w.b_down),
-            10: ((w.b, 0, w.a2), w.a_up),
-            11: ((w.b, 1, w.a2), w.a_down),
-            12: ((w.b, 1, w.ap), w.a_up),
-            13: ((w.b, 0, w.am), w.a_down),
-            14: ((w.b, 0, w.ap), w.a_up),
-            15: ((w.b, 1, w.am), w.a_down),
-            16: ((w.b, w.zo, w.a), w.cross),
-            17: ((w.b, w.zh, w.a), w.pair),
-        }[k]
+        if k >= 13:
+            place, device = {
+                13: ((w.b, w.zo, w.a), w.third),
+                14: ((w.b, w.zo, w.a), w.cross),
+                15: ((w.b, w.zh, w.a), w.pair),
+            }[k]
+            return self.s(c, *place), self.zb.at[w.z], device
+        if self.direct and k < 10:
+            place, device = {4: ((w.b2,), w.b_far), 5: ((w.bp,), w.b_up), 6: ((w.bm,), w.b_down)}[k]
+        else:
+            place, device = {
+                4: ((w.b2, 0), w.b_up),
+                5: ((w.b2, 1), w.b_down),
+                6: ((w.bp, 1), w.b_up),
+                7: ((w.bm, 0), w.b_down),
+                8: ((w.bp, 0), w.b_up),
+                9: ((w.bm, 1), w.b_down),
+                10: ((w.b, every, w.a2), w.a_far),
+                11: ((w.b, every, w.ap), w.a_up),
+                12: ((w.b, every, w.am), w.a_down),
+            }[k]
         return self.s(c, *place), self.lands(k), device
 
     def lands(self, k):
         w = self.w
         if k < 4:
             return self.tw.at[(w.b2, w.bp, w.bm, w.b)[k]]
-        if k == 18:
+        if k == 16:
             return self.done.at[1 - w.core]
+        if k >= 13:
+            return self.zb.at[((w.z + 2) % 4, 3 - w.z, w.zh * 2 + 1 - w.zl)[k - 13]]
+        if self.direct and k < 10:
+            return self.fx.at[(2, 0, 1)[k - 4]]
         return {
-            4: self.r1.at[0],
-            5: self.r1.at[1],
+            4: self.fx.at[2, 0],
+            5: self.fx.at[2, 1],
             6: self.fx.at[0, 1],
             7: self.fx.at[1, 0],
             8: self.fx.at[0, 0],
             9: self.fx.at[1, 1],
-            10: self.ar.at[0],
-            11: self.ar.at[1],
-            12: self.af.at[0, 1],
-            13: self.af.at[1, 0],
-            14: self.af.at[0, 0],
-            15: self.af.at[1, 1],
-            16: self.zr,
-            17: self.pr,
+            10: self.af.at[2],
+            11: self.af.at[0],
+            12: self.af.at[1],
         }[k]
 
     def add(self, place, *terms):
@@ -266,77 +278,57 @@
     def r0(self):
         self.send(0, 1, 2, 3)
 
-    def r1_(self):
+    def r1(self):
         w = self.w
-        self.take(0)
-        self.add8(w.b2, self.tw.at[w.b2])
-        self.send(4, 5)
-        self.take(1)
-        self.add8(w.bp, self.tw.at[w.bp])
-        self.send(6)
-        self.take(2)
-        self.add8(w.bm, self.tw.at[w.bm])
-        self.send(7)
+        for k, b in enumerate((w.b2, w.bp, w.bm)):
+            self.take(k)
+            self.add8(b, self.tw.at[b])
+            self.send(*((4 + k,) if self.direct else ((4, 5), (6,), (7,))[k]))
 
     def r2(self):
         w = self.w
         self.take(3)
         self.add8(w.b, self.tw.at[w.b])
-        self.take(4)
-        self.add4(w.bp, 0, self.r1.at[0])
-        self.send(8)
-        self.take(5)
-        self.add4(w.bm, 1, self.r1.at[1])
-        self.send(9)
+        if not self.direct:
+            self.take(4)
+            self.add4(w.bp, 0, self.fx.at[2, 0])
+            self.send(8)
+            self.take(5)
+            self.add4(w.bm, 1, self.fx.at[2, 1])
+            self.send(9)
 
     def r3(self):
-        self.take(6, 7, 8, 9)
-        self.add8(self.w.b, self.fx.at[0], self.fx.at[1])
-        self.send(10, 11, 12, 13)
+        if self.direct:
+            self.take(4, 5, 6)
+            self.add8(self.w.b, self.fx.at[0], self.fx.at[1], self.fx.at[2])
+        else:
+            self.take(6, 7, 8, 9)
+            self.add8(self.w.b, self.fx.at[0], self.fx.at[1])
+        self.send(10, 11, 12)
 
     def r4(self):
         w = self.w
-        self.take(10, 11)
-        self.add((w.b, 0, w.ap), self.ar.at[0])
-        self.send(14)
-        self.add((w.b, 1, w.am), self.ar.at[1])
-        self.send(15)
+        self.take(10, 11, 12)
+        for z in range(2):
+            self.add((w.b, z, w.a), self.af.at[0, z], self.af.at[1, z], self.af.at[2, z])
+        self.send(13, 14, 15)
+        self.zb[w.z] = self.s(w.core, w.b, w.zh, w.a)[...]
 
     def r5(self):
-        w = self.w
-        self.take(12, 13, 14, 15)
-        for z in range(2):
-            self.add((w.b, z, w.a), self.af.at[0, z], self.af.at[1, z])
+        self.take(13, 14, 15)
+        self.done[self.w.core] = sum(self.zb[i].astype(F32) for i in range(4))
         self.send(16)
 
     def r6(self):
-        w = self.w
         self.take(16)
-        self.add((w.b, w.zh, w.a), self.zr)
-        self.send(17)
-
-    def r7(self):
-        w = self.w
-        self.take(17)
-        self.done[w.core] = self.s(w.core, w.b, w.zh, w.a)[...].astype(F32) + self.pr[...].astype(F32)
-        self.send(18)
-
-    def r8(self):
-        self.take(18)
-
-
-STAGES = ("r0", "r1_", "r2", "r3", "r4", "r5", "r6", "r7", "r8")
 
 
 def reduce_scratch(rows, half):
     return [
         pltpu.VMEM((4, 2, 4, rows, half), BF),
-        pltpu.VMEM((2, 4, rows, half), BF),
-        pltpu.VMEM((2, 2, 4, rows, half), BF),
-        pltpu.VMEM((2, rows, half), BF),
-        pltpu.VMEM((2, 2, rows, half), BF),
-        pltpu.VMEM((rows, half), BF),
-        pltpu.VMEM((rows, half), BF),
+        pltpu.VMEM((3, 2, 4, rows, half), BF),
+        pltpu.VMEM((3, 2, rows, half), BF),
+        pltpu.VMEM((4, rows, half), BF),
         pltpu.VMEM((2, rows, half), F32),
     ]
 
@@ -411,28 +403,47 @@
 
 
 def kernel(
-    tokens, lengths, pads, og, in_shard, out_shard, up_shard, down_shard,
+    tokens_in, lengths, pads, og_in, in_weight, out_weight, up_weight, down_weight,
+    v0, v1, v2, v3, v4, v5, v6, v7, v8,
     layer_out, input_grad, d_in, d_out, d_up, d_down, d_small,
-    raw_in, raw_out, raw_up, raw_down, small, w_in, w_out, w_up, w_down,
-    h1, joint, lse, attended, residual, h2, h2t, dh2, vec, ub, gvec, dub,
-    gs, gr, rs, rr, *bufs,
+    tokens, og, in_pack, vpack, raw_in, raw_out, raw_up, raw_down, small, w_in, w_out, w_up, w_down,
+    h1, joint, lse, attended, residual, h2, h2t, dh2, acc, slope, vec, ub, gvec, dub,
+    ls, gs, gr, rs, rr, *bufs,
 ):
     w = Where()
     w.greet()
+    loads = [
+        pltpu.make_async_copy(src, dst, ls.at[i])
+        for i, (src, dst) in enumerate(
+            (
+                (in_weight.at[:, 0:1152], in_pack.at[:, 0:1152]),
+                (in_weight.at[:, 1152:2304], in_pack.at[:, 1280:2432]),
+                (tokens_in, tokens),
+                (og_in, og),
+            )
+        )
+    ]
+    for load in loads:
+        load.start()
     gq, go, gu, gd = [
-        Gather(w, s, r, gs.at[i], gr.at[i])
+        Gather(w, s, r, i == 0, ls.at[4 + i], gs.at[i], gr.at[i])
         for i, (s, r) in enumerate(
-            ((in_shard, raw_in), (out_shard, raw_out), (up_shard, raw_up), (down_shard, raw_down))
+            ((in_pack, raw_in), (out_weight, raw_out), (up_weight, raw_up), (down_weight, raw_down))
         )
     ]
     every = (gq, go, gu, gd)
-    places = [(raw_up, 0), (raw_up, 768), (raw_down, 0), (raw_out, 0)]
-    places += [(raw_in, 0), (raw_in, 384), (raw_in, 768), (small, 0)]
+    places = [(raw_up, 0, False), (raw_up, 768, False), (raw_down, 0, False), (raw_out, 0, False)]
+    places += [(raw_in, 0, False), (raw_in, 384, False), (raw_in, 768, True), (small, 0, True)]
     ru0, ru1, rd, ro, rq0, rq1, rq2, rv = [
-        Reduce(w, part, first, bufs[8 * i : 8 * i + 8], rs.at[i], rr.at[i])
-        for i, (part, first) in enumerate(places)
+        Reduce(w, part, first, direct, bufs[5 * i : 5 * i + 5], rs.at[i], rr.at[i])
+        for i, (part, first, direct) in enumerate(places)
     ]
-
+    vpack[...] = jnp.zeros_like(vpack)
+    for j, v in enumerate((v0, v1, v2, v3, v4, v5, v6, v7)):
+        vpack[j : j + 1, 0:24] = v[...].astype(F32)
+    vpack[8:9, 0:96] = v8[...].astype(F32)
+    in_pack[:, 1152:1280] = vpack[...].astype(BF)
+    in_pack[:, 2432:2560] = jnp.zeros((24, SMALL), BF)
     gvec[...] = jnp.zeros_like(gvec)
 
     def codes(dim):
@@ -444,21 +455,31 @@
             start = start + lengths[0, j]
         return jnp.where(pos < ROWS - pads[0, 0], seg, -1 - pos)
 
+    loads[0].wait()
+    loads[1].wait()
     w.meet()
     for g in every:
         g.g0()
-    for g in every:
-        g.g1()
-    for g in every:
-        g.g2()
-    for g in every:
-        g.g3()
+
+    loads[2].wait()
+    loads[3].wait()
+
+    def norm_one(rows, c):
+        residual[rows, :] = stats(tokens[rows, :].astype(F32))[0]
+        return c
+
+    lax.fori_loop(0, 4, row_blocks(4, norm_one), 0)
+    for g in (go, gu, gd):
+        g.g0a()
+    gq.g1()
+    for g in (go, gu, gd):
+        g.g0b()
+    go.g1()
+    gq.g2()
+    gu.g1()
+    gd.g1()
+    gq.g3()
     gq.g4()
-    gq.g5()
-    go.g4()
-    gu.g4()
-    gd.g4()
-    gq.g6()
     assemble(raw_in, w_in, 1152)
 
     packed = raw_in[0, :, :, :, 0:16, 1152:1280].reshape(32 * 16, SMALL)
@@ -471,12 +492,7 @@
     n, row = iota((32, FF), 1), iota((32, FF), 0)
     ub[...] = column_sum(jnp.where(lax.shift_right_logical(by24(n), 2) == row, spread, 0.0))
 
-    def norm_one(rows, c):
-        normed, _ = stats(tokens[rows, :].astype(F32))
-        h1[rows, :] = (normed * vec[0:1, :] + vec[1:2, :]).astype(BF)
-        return c
-
-    lax.fori_loop(0, 4, row_blocks(4, norm_one), 0)
+    h1[...] = (residual[...] * vec[0:1, :] + vec[1:2, :]).astype(BF)
 
     for t in range(3):
         bias = (vec[2:3, :], jnp.zeros((1, D), F32), vec[3:4, :])[t]
@@ -510,23 +526,19 @@
             mixed = o if first == 0 else jnp.where(lane < 64, mixed, o)
         attended[:, cq] = mixed.astype(BF)
 
-        @pl.when(p == 0)
-        def _():
-            go.g5()
-
-        @pl.when(p == 1)
-        def _():
-            gu.g5()
-
-        @pl.when(p == 3)
-        def _():
-            gd.g5()
+        plan = ((go.g2,), (gu.g2,), (go.g3,), (gd.g2,), (gu.g3,), (gd.g3,))
+        for i, stages in enumerate(plan):
+
+            @pl.when(p == i)
+            def _(stages=stages):
+                for stage in stages:
+                    stage()
 
         return c
 
     lax.fori_loop(0, 6, attend, 0)
 
-    go.g6()
+    go.g4()
     assemble(raw_out, w_out, TILE)
     for u in range(2):
         columns = slice(u * TILE, (u + 1) * TILE)
@@ -541,56 +553,62 @@
 
     lax.fori_loop(0, 4, row_blocks(4, norm_two), 0)
     h2t[...] = h2[...].T
-    gu.g6()
+    gu.g4()
     assemble(raw_up, w_up, 1536)
-    gd.g6()
+    gd.g4()
     assemble(raw_down, w_down, TILE)
     for g in every:
         g.end()
 
-    input_grad[...] = residual[...] + vec[7:8, :]
-    dh2[...] = jnp.zeros_like(dh2)
-
-    def tile(i, c):
-        t = i // 2 + 4 * (i % 2)
+    acc[...] = residual[...] + vec[7:8, :]
+
+    def forth(t, c):
         columns = pl.ds(pl.multiple_of(t * TILE, TILE), TILE)
         u = nn(h2[...], w_up[:, columns]) + ub[:, columns]
         k = 0.7978845608028654
-        th = jnp.tanh(k * (u + 0.044715 * (u * u * u)))
+        square = u * u
+        th = jnp.tanh(u * (k + (k * 0.044715) * square))
         low = 0.5 * (1.0 + th)
         act = (u * low).astype(BF)
-        slope = low + (0.5 * k) * u * (1.0 - th * th) * (1.0 + (3 * 0.044715) * (u * u))
-        down = w_down[columns, :]
-        input_grad[...] += nn(act, down)
-        grad_pre = (nt(og[...], down) * slope).astype(BF)
-        dub[:, columns] = column_sum(grad_pre.astype(F32))
-        scatter_rows(nn(h2t[...], grad_pre), raw_up, t // 4, pl.multiple_of((t % 4) * TILE, 128))
-        dh2[...] += nt(grad_pre, w_up[:, columns])
+        slope[:, columns] = (
+            low + u * (1.0 - th * th) * (0.5 * k + (1.5 * 0.044715 * k) * square)
+        ).astype(BF)
+        acc[...] += nn(act, w_down[columns, :])
         grad_down = tn(act, og[...]).astype(BF)
         x, z = t // 2, t % 2
         for y in range(4):
             raw_down[0, x, z, y] = grad_down[96 * y : 96 * y + 96, :TILE]
             raw_down[1, y, z, x] = grad_down[96 * y : 96 * y + 96, TILE:]
-
-        @pl.when(i == 3)
-        def _():
-            ru0.r0()
-
-        @pl.when(i == 4)
-        def _():
-            ru0.r1_()
-
-        @pl.when(i == 5)
-        def _():
-            ru0.r2()
-
         return c
 
-    lax.fori_loop(0, 8, tile, 0)
+    lax.fori_loop(0, 8, forth, 0)
     rd.r0()
+    h2[...] = acc[...].astype(BF)
+    out_copy = pltpu.make_async_copy(h2, layer_out, ls.at[8])
+    out_copy.start()
+
+    dh2[...] = jnp.zeros_like(dh2)
+
+    def back(i, c):
+        t = i // 2 + 4 * (i % 2)
+        columns = pl.ds(pl.multiple_of(t * TILE, TILE), TILE)
+        grad_pre = (nt(og[...], w_down[columns, :]) * slope[:, columns].astype(F32)).astype(BF)
+        dub[:, columns] = column_sum(grad_pre.astype(F32))
+        scatter_rows(nn(h2t[...], grad_pre), raw_up, t // 4, pl.multiple_of((t % 4) * TILE, 128))
+        dh2[...] += nt(grad_pre, w_up[:, columns])
+        plan = {1: (rd.r1,), 3: (ru0.r0,), 4: (rd.r2,), 5: (ru0.r1,), 7: (rd.r3,)}
+        for j, stages in plan.items():
+
+            @pl.when(i == j)
+            def _(stages=stages):
+                for stage in stages:
+                    stage()
+
+        return c
+
+    lax.fori_loop(0, 8, back, 0)
     ru1.r0()
-    ru0.r3()
-    layer_out[...] = input_grad[...].astype(BF)
+    ru0.r2()
 
     def back_two(rows, c):
         normed, inv = stats(residual[rows, :])
@@ -611,7 +629,7 @@
     sums = lax.fori_loop(0, 4, row_blocks(4, back_two), (zero, zero, zero, zero))
     for j, v in zip((4, 5, 6, 7), sums):
         gvec[j : j + 1, :] = v
-    rd.r1_()
+    ru1.r1()
     grad_branch = w_up.at[0:ROWS, 0:D]
     grad_attended = w_up.at[0:ROWS, D : 2 * D]
     for u in range(2):
@@ -619,9 +637,8 @@
         scatter_rows(tn(attended[...], grad_branch[:, columns]), raw_out, u, 0)
         grad_attended[:, columns] = nt(grad_branch[...], w_out[columns, :]).astype(BF)
     ro.r0()
-    ru1.r1_()
-    rd.r2()
-    ru0.r4()
+    rd.r4()
+    ru0.r3()
     h1t = h2t
     h1t[...] = h1[...].T
 
@@ -651,12 +668,12 @@
         both = jnp.concatenate([dq, dk, dv], axis=1)
         scatter_rows(nn(h1t[...], both), raw_in, p % 2, pl.multiple_of((p // 2) * TILE, 128))
         plan = (
-            (ro.r1_, ru1.r2, rd.r3, ru0.r5),
-            (rq0.r0, ro.r2, ru1.r3, rd.r4, ru0.r6),
-            (rq0.r1_, ro.r3, ru1.r4, rd.r5, ru0.r7),
-            (rq1.r0, rq0.r2, ro.r4, ru1.r5, rd.r6, ru0.r8),
-            (rq1.r1_, rq0.r3, ro.r5, ru1.r6, rd.r7),
-            (rq2.r0, rq1.r2, rq0.r4, ro.r6, ru1.r7, rd.r8),
+            (ro.r1, ru1.r2),
+            (rq0.r0, ru0.r4, rd.r5),
+            (ro.r2, rq0.r1, ru1.r3, rd.r6),
+            (rq1.r0, ro.r3, rq0.r2, ru0.r5),
+            (rq1.r1, ru1.r4, ro.r4, ru0.r6),
+            (rq2.r0, rq0.r3, rq1.r2),
         )
         for i, stages in enumerate(plan):
 
@@ -669,25 +686,28 @@
 
     lax.fori_loop(0, 6, attend_back, 0)
 
-    rq2.r1_()
+    rq2.r1()
     for u in range(2):
         columns = slice(u * TILE, (u + 1) * TILE)
         dh2[:, columns] = nt(joint[...], w_in[columns, :])
     rq2.r2()
     rq1.r3()
-    rq0.r5()
-    ro.r7()
-    ru1.r8()
+    ru1.r5()
+    rq0.r4()
+    ro.r5()
 
     def back_one(rows, c):
         normed, inv = stats(tokens[rows, :].astype(F32))
         grad = dh2[rows, :]
-        input_grad[rows, :] = residual[rows, :] + norm_backward(grad, normed, inv, vec[0:1, :])
+        acc[rows, :] = residual[rows, :] + norm_backward(grad, normed, inv, vec[0:1, :])
         return c[0] + column_sum(grad * normed), c[1] + column_sum(grad)
 
     sums = lax.fori_loop(0, 4, row_blocks(4, back_one), (zero, zero))
+    grad_copy = pltpu.make_async_copy(acc, input_grad, ls.at[9])
+    grad_copy.start()
     for j, v in zip((0, 1), sums):
         gvec[j : j + 1, :] = v
+    rq2.r3()
 
     n, row = iota((32, 16, D), 2), iota((32, 16, D), 0)
     spread = jnp.where(by24(n) == row, jnp.broadcast_to(gvec[...][None], (32, 16, D)), 0.0)
@@ -700,29 +720,22 @@
         small[0, x, z, y] = own[f]
         small[1, y, z, x] = jnp.broadcast_to(hidden[f : f + 1], (16, SMALL)).astype(BF)
     rv.r0()
-    rq2.r3()
     rq1.r4()
-    rv.r1_()
-    rq0.r6()
-    ro.r8()
+    rv.r1()
+    rq0.r5()
     rv.r2()
     rq2.r4()
+    rv.r3()
     rq1.r5()
-    rv.r3()
-    rq0.r7()
+    ru1.r6()
+    ro.r6()
     rq2.r5()
     rv.r4()
+    rq0.r6()
     rq1.r6()
-    rq0.r8()
+    rv.r5()
     rq2.r6()
-    rv.r5()
-    rq1.r7()
     rv.r6()
-    rq2.r7()
-    rq1.r8()
-    rv.r7()
-    rq2.r8()
-    rv.r8()
 
     for h in range(2):
         d_up[:, h * 1536 : h * 1536 + 768] = ru0.done[h]
@@ -736,6 +749,25 @@
                 d_in[:, to : to + 128] = r.done[h, :, 128 * j : 128 * j + 128]
     for r in (ru0, ru1, rd, ro, rq0, rq1, rq2, rv):
         r.end()
+    out_copy.wait()
+    grad_copy.wait()
+
+
+def finish(*refs):
+    packed, src, dst, vectors = refs[6], refs[:6], refs[7:13], refs[13:22]
+    held, taken, given = refs[22:28], refs[28], refs[29]
+    arrive = [pltpu.make_async_copy(s, h, taken.at[i]) for i, (s, h) in enumerate(zip(src, held))]
+    leave = [pltpu.make_async_copy(h, d, given.at[i]) for i, (h, d) in enumerate(zip(held, dst))]
+    for c in arrive:
+        c.start()
+    for j in range(8):
+        vectors[j][...] = packed[0, j : j + 1, 0:24]
+    vectors[8][...] = packed[1, 0:1, 0:96]
+    for c, d in zip(arrive, leave):
+        c.wait()
+        d.start()
+    for c in leave:
+        c.wait()
 
 
 def shards(
@@ -743,18 +775,14 @@
     value_bias, output_weight, output_bias, second_gain, second_shift, up_weight, up_bias, down_weight,
     down_bias,
 ):
-    vectors = jnp.stack(
-        [first_gain, first_shift, query_bias, value_bias, output_bias, second_gain, second_shift, down_bias]
-    )
-    vectors = jnp.pad(vectors, ((0, 0), (0, SMALL - 24)))
-    hidden = jnp.pad(up_bias[None], ((0, 15), (0, SMALL - 96)))
-    packed = jnp.concatenate([vectors, hidden], axis=0)
-    in_shard = jnp.concatenate(
-        [input_weight[:, :1152], packed, input_weight[:, 1152:], jnp.zeros((24, SMALL), BF)], axis=1
-    )
     vmem = pl.BlockSpec(memory_space=pltpu.VMEM)
     smem = pl.BlockSpec(memory_space=pltpu.SMEM)
+    hbm = pl.BlockSpec(memory_space=pl.ANY)
     scratch = [
+        pltpu.VMEM((ROWS, D), BF),
+        pltpu.VMEM((ROWS, D), BF),
+        pltpu.VMEM((24, 2560), BF),
+        pltpu.VMEM((24, SMALL), F32),
         pltpu.VMEM((2, 4, 2, 4, 24, 1280), BF),
         pltpu.VMEM((2, 4, 2, 4, 24, 384), BF),
         pltpu.VMEM((2, 4, 2, 4, 24, 1536), BF),
@@ -772,43 +800,63 @@
         pltpu.VMEM((ROWS, D), BF),
         pltpu.VMEM((D, ROWS), BF),
         pltpu.VMEM((ROWS, D), F32),
+        pltpu.VMEM((ROWS, D), F32),
+        pltpu.VMEM((ROWS, FF), BF),
         pltpu.VMEM((16, D), F32),
         pltpu.VMEM((1, FF), F32),
         pltpu.VMEM((16, D), F32),
         pltpu.VMEM((1, FF), F32),
+        pltpu.SemaphoreType.DMA((10,)),
         pltpu.SemaphoreType.DMA((4, 16)),
         pltpu.SemaphoreType.DMA((4, 16)),
-        pltpu.SemaphoreType.DMA((8, 19)),
-        pltpu.SemaphoreType.DMA((8, 19)),
+        pltpu.SemaphoreType.DMA((8, 17)),
+        pltpu.SemaphoreType.DMA((8, 17)),
     ]
     for rows, half in ((24, 768), (24, 768), (96, 384), (24, 384), (24, 384), (24, 384), (24, 384), (16, SMALL)):
         scratch += reduce_scratch(rows, half)
     shape = jax.ShapeDtypeStruct
-    layer_out, input_grad, d_in, d_out, d_up, d_down, d_small = pl.pallas_call(
+    large = [
+        shape((ROWS, D), BF),
+        shape((ROWS, D), F32),
+        shape((24, 3 * D), F32),
+        shape((24, D), F32),
+        shape((24, FF), F32),
+        shape((96, D), F32),
+    ]
+    vectors = (
+        first_gain, first_shift, query_bias, value_bias, output_bias, second_gain, second_shift, down_bias,
+        up_bias,
+    )
+    results = pl.pallas_call(
         kernel,
-        out_shape=[
-            shape((ROWS, D), BF),
-            shape((ROWS, D), F32),
-            shape((24, 3 * D), F32),
-            shape((24, D), F32),
-            shape((24, FF), F32),
-            shape((96, D), F32),
-            shape((2, 16, SMALL), F32),
-        ],
-        in_specs=[vmem, smem, smem, vmem, vmem, vmem, vmem, vmem],
-        out_specs=[vmem] * 7,
+        out_shape=[*large, shape((2, 16, SMALL), F32)],
+        in_specs=[hbm, smem, smem, hbm, hbm, hbm, hbm, hbm, *[vmem] * 9],
+        out_specs=[hbm, hbm, *[vmem] * 5],
         scratch_shapes=scratch,
         compiler_params=pltpu.CompilerParams(
             collective_id=0, has_side_effects=True, vmem_limit_bytes=63 << 20
         ),
         cost_estimate=pl.CostEstimate(flops=25 * 10**9, bytes_accessed=6 * 10**6, transcendentals=8 * 10**6),
     )(
-        tokens, image_lengths, pad_counts.reshape(1, 1), out_grad, in_shard, output_weight, up_weight, down_weight
+        tokens, image_lengths, pad_counts.reshape(1, 1), out_grad, input_weight, output_weight, up_weight,
+        down_weight, *[v.reshape(1, -1) for v in vectors],
     )
-    v = [d_small[0, j, :24] for j in range(8)]
+    done = pl.pallas_call(
+        finish,
+        out_shape=[*large, *[shape((1, v.shape[0]), F32) for v in vectors]],
+        in_specs=[*[hbm] * 6, vmem],
+        out_specs=[*[hbm] * 6, *[vmem] * 9],
+        scratch_shapes=[
+            *[pltpu.VMEM(x.shape, x.dtype) for x in large],
+            pltpu.SemaphoreType.DMA((6,)),
+            pltpu.SemaphoreType.DMA((6,)),
+        ],
+    )(*results)
+    layer_out, input_grad, d_in, d_out, d_up, d_down = done[:6]
+    v = [x.reshape(-1) for x in done[6:]]
     return (
-        layer_out, input_grad, v[0], v[1], d_in, v[2], v[3], d_out, v[4], v[5], v[6], d_up,
-        d_small[1, 0, :96], d_down, v[7],
+        layer_out, input_grad, v[0], v[1], d_in, v[2], v[3], d_out, v[4], v[5], v[6], d_up, v[8], d_down,
+        v[7],
     )
 
 

time: 172 us -> 153 us (0.89)
  local copies, waits for them, and re-layouts: 10.5 us -> 0 us
  Pallas kernels: 159 us -> 151 us
    pallas_call x1 -> x2, Pallas kernels: 159 us -> 151 us  [the longest x1 147 us: shards(): pl.pallas_call(kernel, out_shape=[*large, shape((2, 16, SMALL), F32)], in...]
    unnamed x16 -> x0, local copies, waits for them, and re-layouts: 5.97 us -> none
    squeeze x2 -> x0, local copies, waits for them, and re-layouts: 2.83 us -> none  [the longest x1 1.52 us: shards(): v = [d_small[0, j, :24] for j in range(8)]]
where the time goes in v2:
time: 153 us
  Pallas kernels  151 us (99%)
    pallas_call x1, Pallas kernels, shards(): pl.pallas_call(kernel, out_shape=[*large, shape((2, 16, SMALL), F32)], in...  147 us
    pallas_call x1, Pallas kernels, shards(): pl.pallas_call(finish, out_shape=[*large, *[shape((1, v.shape[0]), F32) f...  4.46 us

profile of v2, /device:TPU:1, one launch (start us, length us, event | category | flops | bytes accessed | tf_op | source)
XLA Modules:
  0.0 152.8 jit_solution(5840174557602983754)
XLA Ops:
  1.3 146.8 %shard_map.280 = (bf16[512,768]{1,0:T(8,128)(2,1)}, f32[512,768]{1,0:T(8,128)}, f32[24,2304]{1,0:T(8,128)}, f32[24,768]{1,0:T(8,128)}, f32[24,3072]{1,0:T(8,128)...) custom-call(bf16[512,768]{1,0:T(8,128)(2,1)} %tokens_in.1, s32[1,6]{1,0:T(1,128)} %lengths.1, s32[1,1]{1,0:T(1,128)} %bitcast.19.pads, ...), custom_call_target="tpu_custom_call" | custom-call | flops 24999999488 | bytes 6000000 | tf_op jit(solution)/shard_map/pallas_call | solution.py:830
  148.2 4.5 %shard_map.281 = (bf16[512,768]{1,0:T(8,128)(2,1)}, f32[512,768]{1,0:T(8,128)}, f32[24,2304]{1,0:T(8,128)}, f32[24,768]{1,0:T(8,128)}, f32[24,3072]{1,0:T(8,128)...) custom-call(bf16[512,768]{1,0:T(8,128)(2,1)} %get-tuple-element.37.r, ...), custom_call_target="tpu_custom_call" | custom-call | tf_op jit(solution)/shard_map/pallas_call | solution.py:844

commit v3 on v2

--- a/solution.py
+++ b/solution.py
@@ -15,6 +15,7 @@
 TILE = 384
 SMALL = 128
 LOW = -1e30
+SLOPE = 0.7978845608028654
 
 
 def nn(left, right):
@@ -46,6 +47,7 @@
         self.z = self.zh * 2 + self.zl
         self.twin = {"rep": self.r + 1 - 2 * c, "fsdp": self.f}
         self.pair = {"rep": (1 - self.zl) * 2 + c, "fsdp": self.f}
+        self.diagonal = {"rep": (1 - self.zl) * 2 + 1 - c, "fsdp": self.f}
         self.cross, self.cross_up, self.cross_down, self.cross_far = [self.over(i) for i in (0, 1, 3, 2)]
         self.third = {"rep": self.r, "fsdp": (self.x * 2 + self.zo) * 4 + self.y}
 
@@ -63,7 +65,7 @@
 
     def friends(self):
         near = [self.a_up, self.a_down, self.a_far, self.b_up, self.b_down, self.b_far, self.twin]
-        return near + [self.pair, self.third, self.cross, self.cross_up, self.cross_down, self.cross_far]
+        return near + [self.pair, self.diagonal, self.third, self.cross, self.cross_up, self.cross_down, self.cross_far]
 
     def greet(self):
         sem = pltpu.get_barrier_semaphore()
@@ -183,6 +185,91 @@
 
     def g4(self):
         self.take(11, 12, 13, 14, 15)
+
+
+class GatherZ(Copies):
+    count = 23
+
+    def __init__(self, w, src, raw, local, ss, rs):
+        self.w, self.src, self.raw, self.ss, self.rs = w, src, raw, ss, rs
+        self.half, self.part = src.shape[1] // 2, src.shape[0] // 2
+        self.rows = (w.b, w.bm, w.bp, w.b2)
+        self.local = pltpu.make_async_copy(self.own(), self.slot(w.core, w.b, w.zh, w.a, w.zl), local)
+
+    def quarter(self, q):
+        return pl.ds(pl.multiple_of(q * self.part, 16), self.part)
+
+    def own(self):
+        w = self.w
+        return self.src.at[self.quarter(w.zl), pl.ds(pl.multiple_of(w.core * self.half, 128), self.half)]
+
+    def slot(self, h, b, z, a, q):
+        return self.raw.at[h, b, z, a, self.quarter(q), :]
+
+    def route(self, k):
+        w, c, every = self.w, self.w.core, slice(None)
+        if k < 3:
+            return self.own(), self.slot(c, w.b, w.zh, w.a, w.zl), (w.a_up, w.a_down, w.a_far)[k]
+        if 7 <= k < 19:
+            here = self.slot(c, self.rows[(k - 7) // 3], w.zh, every, w.zl)
+            return here, here, (w.pair, w.cross, w.third)[(k - 7) % 3]
+        place, device = {
+            3: ((w.b, w.zh, every, w.zl), w.b_up),
+            4: ((w.b, w.zh, every, w.zl), w.b_down),
+            5: ((w.bm, w.zh, slice(0, 2), w.zl), w.b_up),
+            6: ((w.bp, w.zh, slice(2, 4), w.zl), w.b_down),
+            19: ((every, w.zh, every, w.zl), w.twin),
+            20: ((every, w.zh, every, 1 - w.zl), w.twin),
+            21: ((every, w.zo, every, 1 - w.zl), w.twin),
+            22: ((every, w.zo, every, w.zl), w.twin),
+        }[k]
+        here = self.slot(c, *place)
+        return here, here, device
+
+    def lands(self, k):
+        w, c, every = self.w, self.w.core, slice(None)
+        if k < 3:
+            return self.slot(c, w.b, w.zh, (w.am, w.ap, w.a2)[k], w.zl)
+        if 7 <= k < 19:
+            z, q = ((w.zh, 1 - w.zl), (w.zo, 1 - w.zl), (w.zo, w.zl))[(k - 7) % 3]
+            return self.slot(c, self.rows[(k - 7) // 3], z, every, q)
+        return self.slot(
+            *{
+                3: (c, w.bm, w.zh, every, w.zl),
+                4: (c, w.bp, w.zh, every, w.zl),
+                5: (c, w.b2, w.zh, slice(0, 2), w.zl),
+                6: (c, w.b2, w.zh, slice(2, 4), w.zl),
+                19: (1 - c, every, w.zh, every, w.zl),
+                20: (1 - c, every, w.zh, every, 1 - w.zl),
+                21: (1 - c, every, w.zo, every, 1 - w.zl),
+                22: (1 - c, every, w.zo, every, w.zl),
+            }[k]
+        )
+
+    def g0(self):
+        self.send(2, 0, 1)
+        self.local.start()
+
+    def g1(self):
+        self.local.wait()
+        self.take(0, 1, 2)
+        self.send(3, 4, 9, 7, 8)
+
+    def g2(self):
+        self.take(3, 4)
+        self.send(5, 6, 12, 10, 11, 15, 13, 14)
+
+    def g3(self):
+        self.take(5, 6)
+        self.send(18, 16, 17, 19)
+
+    def g3z(self):
+        for d in range(3):
+            self.take(7 + d, 10 + d, 13 + d, 16 + d)
+            self.send(20 + d)
+
+    def g4(self):
+        self.take(19, 20, 21, 22)
 
 
 class Reduce(Copies):
@@ -323,6 +410,127 @@
         self.take(16)
 
 
+class ReduceZ(Copies):
+    def __init__(self, w, part, bufs, ss, rs):
+        self.w, self.part, self.ss, self.rs = w, part, ss, rs
+        self.tw, self.zr, self.fx, self.af, self.done = bufs
+        self.half = self.af.shape[-2]
+        self.rows = (w.b2, w.bp, w.bm, w.b)
+        self.count = 25
+
+    def s(self, b, z, a, q):
+        return self.part.at[
+            self.w.core, b, z, a, pl.ds(pl.multiple_of(q * self.half, 16), self.half), :
+        ]
+
+    def route(self, k):
+        w, c, every = self.w, self.w.core, slice(None)
+        if k < 4:
+            j = (w.a2, w.ap, w.am, w.a)[k]
+            return self.part.at[1 - c, j], self.tw.at[j], w.twin
+        if k < 16:
+            b, d = self.rows[(k - 4) // 3], (k - 4) % 3
+            z, q, device = (
+                (w.zh, 1 - w.zl, w.pair),
+                (w.zo, 1 - w.zl, w.cross),
+                (w.zo, w.zl, w.third),
+            )[d]
+            return self.s(b, z, every, q), self.zr.at[d, b], device
+        if k >= 22:
+            here = self.done.at[c, w.zl]
+            return here, here, (w.twin, w.pair, w.diagonal)[k - 22]
+        b, a, device = {
+            16: (w.b2, every, w.b_far),
+            17: (w.bp, every, w.b_up),
+            18: (w.bm, every, w.b_down),
+            19: (w.b, w.a2, w.a_far),
+            20: (w.b, w.ap, w.a_up),
+            21: (w.b, w.am, w.a_down),
+        }[k]
+        return self.s(b, w.zh, a, w.zl), self.lands(k), device
+
+    def lands(self, k):
+        w, c = self.w, self.w.core
+        if k < 4:
+            return self.tw.at[self.rows[k]]
+        if k < 16:
+            return self.zr.at[(k - 4) % 3, self.rows[(k - 4) // 3]]
+        if k < 22:
+            return (self.fx if k < 19 else self.af).at[(2, 0, 1)[(k - 16) % 3]]
+        return self.done.at[((1 - c, w.zl), (c, 1 - w.zl), (1 - c, 1 - w.zl))[k - 22]]
+
+    def r0(self):
+        self.send(0, 1, 2, 3)
+
+    def r1(self, which=(0, 1, 2, 3)):
+        for i in which:
+            b = self.rows[i]
+            self.take(i)
+
+            def one(j, _, b=b):
+                z, a = j // 4, j % 4
+                here = self.part.at[self.w.core, b, z, a]
+                here[...] = (here[...].astype(F32) + self.tw[b, z, a].astype(F32)).astype(BF)
+                return 0
+
+            lax.fori_loop(0, 8, one, 0)
+            self.send(6 + 3 * i, 4 + 3 * i, 5 + 3 * i)
+
+    def r2(self, which=(0, 1, 2, 3)):
+        w = self.w
+        for i in which:
+            b = self.rows[i]
+            self.take(4 + 3 * i, 5 + 3 * i, 6 + 3 * i)
+
+            def one(a, _, b=b):
+                self.sum_up(self.s(b, w.zh, a, w.zl), *[self.zr.at[d, b, a] for d in range(3)])
+                return 0
+
+            lax.fori_loop(0, 4, one, 0)
+            if i < 3:
+                self.send(16 + i)
+
+    def sum_up(self, here, *terms):
+        total = here[...].astype(F32)
+        for term in terms:
+            total = total + term[...].astype(F32)
+        here[...] = total.astype(BF)
+
+    def r3(self):
+        w = self.w
+        self.take(16, 17, 18)
+
+        def one(a, _):
+            self.sum_up(self.s(w.b, w.zh, a, w.zl), *[self.fx.at[d, a] for d in range(3)])
+            return 0
+
+        lax.fori_loop(0, 4, one, 0)
+        self.send(19, 20, 21)
+
+    def r4(self):
+        w = self.w
+        self.take(19, 20, 21)
+        total = self.s(w.b, w.zh, w.a, w.zl)[...].astype(F32)
+        for d in range(3):
+            total = total + self.af[d].astype(F32)
+        self.done[w.core, w.zl] = total
+        self.send(22, 23, 24)
+
+    def r5(self):
+        self.take(22, 23, 24)
+
+
+def reduce_z_scratch(rows, half):
+    part = rows // 2
+    return [
+        pltpu.VMEM((4, 2, 4, rows, half), BF),
+        pltpu.VMEM((3, 4, 4, part, half), BF),
+        pltpu.VMEM((3, 4, part, half), BF),
+        pltpu.VMEM((3, part, half), BF),
+        pltpu.VMEM((2, 2, part, half), F32),
+    ]
+
+
 def reduce_scratch(rows, half):
     return [
         pltpu.VMEM((4, 2, 4, rows, half), BF),
@@ -393,6 +601,25 @@
     return (n - 96 * lax.shift_right_logical(by24(n), 2) == iota((SMALL, FF), 0)).astype(F32).astype(BF)
 
 
+def gate(u):
+    square = u * u
+    th = jnp.tanh(u * (SLOPE + (SLOPE * 0.044715) * square))
+    return 0.5 + 0.5 * th, th, square
+
+
+def follow(plan, step):
+    for at, stages in plan.items():
+
+        @pl.when(step == at)
+        def _(stages=stages):
+            for stage in stages:
+                stage()
+
+
+def only(stage, i):
+    return lambda: stage((i,))
+
+
 def row_blocks(count, body):
     step = ROWS // count
 
@@ -407,7 +634,7 @@
     v0, v1, v2, v3, v4, v5, v6, v7, v8,
     layer_out, input_grad, d_in, d_out, d_up, d_down, d_small,
     tokens, og, in_pack, vpack, raw_in, raw_out, raw_up, raw_down, small, w_in, w_out, w_up, w_down,
-    h1, joint, lse, attended, residual, h2, h2t, dh2, acc, slope, vec, ub, gvec, dub,
+    h1, joint, lse, attended, residual, h2, h2t, dh2, acc, pre, vec, ub, gvec, dub,
     ls, gs, gr, rs, rr, *bufs,
 ):
     w = Where()
@@ -425,19 +652,19 @@
     ]
     for load in loads:
         load.start()
-    gq, go, gu, gd = [
+    gq, go, gu = [
         Gather(w, s, r, i == 0, ls.at[4 + i], gs.at[i], gr.at[i])
-        for i, (s, r) in enumerate(
-            ((in_pack, raw_in), (out_weight, raw_out), (up_weight, raw_up), (down_weight, raw_down))
-        )
+        for i, (s, r) in enumerate(((in_pack, raw_in), (out_weight, raw_out), (up_weight, raw_up)))
     ]
+    gd = GatherZ(w, down_weight, raw_down, ls.at[7], gs.at[3], gr.at[3])
     every = (gq, go, gu, gd)
-    places = [(raw_up, 0, False), (raw_up, 768, False), (raw_down, 0, False), (raw_out, 0, False)]
+    places = [(raw_up, 0, False), (raw_up, 768, False), (raw_out, 0, False)]
     places += [(raw_in, 0, False), (raw_in, 384, False), (raw_in, 768, True), (small, 0, True)]
-    ru0, ru1, rd, ro, rq0, rq1, rq2, rv = [
+    ru0, ru1, ro, rq0, rq1, rq2, rv = [
         Reduce(w, part, first, direct, bufs[5 * i : 5 * i + 5], rs.at[i], rr.at[i])
         for i, (part, first, direct) in enumerate(places)
     ]
+    rd = ReduceZ(w, raw_down, bufs[35:40], rs.at[7], rr.at[7])
     vpack[...] = jnp.zeros_like(vpack)
     for j, v in enumerate((v0, v1, v2, v3, v4, v5, v6, v7)):
         vpack[j : j + 1, 0:24] = v[...].astype(F32)
@@ -469,15 +696,16 @@
         return c
 
     lax.fori_loop(0, 4, row_blocks(4, norm_one), 0)
-    for g in (go, gu, gd):
-        g.g0a()
+    go.g0a()
+    gu.g0a()
     gq.g1()
-    for g in (go, gu, gd):
-        g.g0b()
+    go.g0b()
+    gu.g0b()
+    gd.g1()
     go.g1()
     gq.g2()
     gu.g1()
-    gd.g1()
+    gd.g2()
     gq.g3()
     gq.g4()
     assemble(raw_in, w_in, 1152)
@@ -526,14 +754,8 @@
             mixed = o if first == 0 else jnp.where(lane < 64, mixed, o)
         attended[:, cq] = mixed.astype(BF)
 
-        plan = ((go.g2,), (gu.g2,), (go.g3,), (gd.g2,), (gu.g3,), (gd.g3,))
-        for i, stages in enumerate(plan):
-
-            @pl.when(p == i)
-            def _(stages=stages):
-                for stage in stages:
-                    stage()
-
+        plan = ((gd.g3,), (go.g2,), (gu.g2,), (go.g3,), (), (gu.g3,))
+        follow(dict(enumerate(plan)), p)
         return c
 
     lax.fori_loop(0, 6, attend, 0)
@@ -555,25 +777,18 @@
     h2t[...] = h2[...].T
     gu.g4()
     assemble(raw_up, w_up, 1536)
+    gd.g3z()
     gd.g4()
     assemble(raw_down, w_down, TILE)
     for g in every:
         g.end()
 
-    acc[...] = residual[...] + vec[7:8, :]
 
     def forth(t, c):
         columns = pl.ds(pl.multiple_of(t * TILE, TILE), TILE)
         u = nn(h2[...], w_up[:, columns]) + ub[:, columns]
-        k = 0.7978845608028654
-        square = u * u
-        th = jnp.tanh(u * (k + (k * 0.044715) * square))
-        low = 0.5 * (1.0 + th)
-        act = (u * low).astype(BF)
-        slope[:, columns] = (
-            low + u * (1.0 - th * th) * (0.5 * k + (1.5 * 0.044715 * k) * square)
-        ).astype(BF)
-        acc[...] += nn(act, w_down[columns, :])
+        pre[:, columns] = u.astype(BF)
+        act = (u * gate(u)[0]).astype(BF)
         grad_down = tn(act, og[...]).astype(BF)
         x, z = t // 2, t % 2
         for y in range(4):
@@ -583,31 +798,31 @@
 
     lax.fori_loop(0, 8, forth, 0)
     rd.r0()
-    h2[...] = acc[...].astype(BF)
-    out_copy = pltpu.make_async_copy(h2, layer_out, ls.at[8])
-    out_copy.start()
-
     dh2[...] = jnp.zeros_like(dh2)
 
     def back(i, c):
         t = i // 2 + 4 * (i % 2)
         columns = pl.ds(pl.multiple_of(t * TILE, TILE), TILE)
-        grad_pre = (nt(og[...], w_down[columns, :]) * slope[:, columns].astype(F32)).astype(BF)
+        u = pre[:, columns].astype(F32)
+        low, th, square = gate(u)
+        slope = low + u * (1.0 - th * th) * (0.5 * SLOPE + (1.5 * 0.044715 * SLOPE) * square)
+        grad_pre = (nt(og[...], w_down[columns, :]) * slope).astype(BF)
         dub[:, columns] = column_sum(grad_pre.astype(F32))
         scatter_rows(nn(h2t[...], grad_pre), raw_up, t // 4, pl.multiple_of((t % 4) * TILE, 128))
         dh2[...] += nt(grad_pre, w_up[:, columns])
-        plan = {1: (rd.r1,), 3: (ru0.r0,), 4: (rd.r2,), 5: (ru0.r1,), 7: (rd.r3,)}
-        for j, stages in plan.items():
-
-            @pl.when(i == j)
-            def _(stages=stages):
-                for stage in stages:
-                    stage()
-
+        plan = {
+            1: (only(rd.r1, 0),),
+            2: (only(rd.r1, 1),),
+            3: (ru0.r0, only(rd.r1, 2)),
+            4: (only(rd.r1, 3),),
+            6: (ru0.r1,),
+        }
+        follow(plan, i)
         return c
 
     lax.fori_loop(0, 8, back, 0)
     ru1.r0()
+    rd.r2((0,))
     ru0.r2()
 
     def back_two(rows, c):
@@ -615,7 +830,7 @@
         grad = dh2[rows, :]
         up = og[rows, :].astype(F32)
         total = up + norm_backward(grad, normed, inv, vec[5:6, :])
-        residual[rows, :] = total
+        acc[rows, :] = total
         rounded = total.astype(BF)
         w_up[rows, 0:D] = rounded
         return (
@@ -637,7 +852,7 @@
         scatter_rows(tn(attended[...], grad_branch[:, columns]), raw_out, u, 0)
         grad_attended[:, columns] = nt(grad_branch[...], w_out[columns, :]).astype(BF)
     ro.r0()
-    rd.r4()
+    rd.r2((1,))
     ru0.r3()
     h1t = h2t
     h1t[...] = h1[...].T
@@ -669,19 +884,13 @@
         scatter_rows(nn(h1t[...], both), raw_in, p % 2, pl.multiple_of((p // 2) * TILE, 128))
         plan = (
             (ro.r1, ru1.r2),
-            (rq0.r0, ru0.r4, rd.r5),
-            (ro.r2, rq0.r1, ru1.r3, rd.r6),
-            (rq1.r0, ro.r3, rq0.r2, ru0.r5),
-            (rq1.r1, ru1.r4, ro.r4, ru0.r6),
-            (rq2.r0, rq0.r3, rq1.r2),
+            (rq0.r0, ru0.r4, only(rd.r2, 2)),
+            (rq0.r1, ro.r2, ru1.r3, ru0.r5),
+            (rq1.r0, rq0.r2, ro.r3, ru1.r4, only(rd.r2, 3)),
+            (rq1.r1, rq0.r3, ro.r4, ru0.r6),
+            (rq2.r0, rd.r3, rq1.r2, ru1.r5, rq0.r4),
         )
-        for i, stages in enumerate(plan):
-
-            @pl.when(p == i)
-            def _(stages=stages):
-                for stage in stages:
-                    stage()
-
+        follow(dict(enumerate(plan)), p)
         return c
 
     lax.fori_loop(0, 6, attend_back, 0)
@@ -690,24 +899,15 @@
     for u in range(2):
         columns = slice(u * TILE, (u + 1) * TILE)
         dh2[:, columns] = nt(joint[...], w_in[columns, :])
-    rq2.r2()
-    rq1.r3()
-    ru1.r5()
-    rq0.r4()
-    ro.r5()
-
-    def back_one(rows, c):
-        normed, inv = stats(tokens[rows, :].astype(F32))
+
+    def sums_one(rows, c):
+        normed, _ = stats(tokens[rows, :].astype(F32))
         grad = dh2[rows, :]
-        acc[rows, :] = residual[rows, :] + norm_backward(grad, normed, inv, vec[0:1, :])
         return c[0] + column_sum(grad * normed), c[1] + column_sum(grad)
 
-    sums = lax.fori_loop(0, 4, row_blocks(4, back_one), (zero, zero))
-    grad_copy = pltpu.make_async_copy(acc, input_grad, ls.at[9])
-    grad_copy.start()
+    sums = lax.fori_loop(0, 4, row_blocks(4, sums_one), (zero, zero))
     for j, v in zip((0, 1), sums):
         gvec[j : j + 1, :] = v
-    rq2.r3()
 
     n, row = iota((32, 16, D), 2), iota((32, 16, D), 0)
     spread = jnp.where(by24(n) == row, jnp.broadcast_to(gvec[...][None], (32, 16, D)), 0.0)
@@ -720,27 +920,50 @@
         small[0, x, z, y] = own[f]
         small[1, y, z, x] = jnp.broadcast_to(hidden[f : f + 1], (16, SMALL)).astype(BF)
     rv.r0()
+    rq2.r2()
+    rd.r4()
+    rq1.r3()
+    ro.r5()
+    rv.r1()
+    rv.r2()
+
+    def back_one(rows, c):
+        normed, inv = stats(tokens[rows, :].astype(F32))
+        acc[rows, :] = acc[rows, :] + norm_backward(dh2[rows, :], normed, inv, vec[0:1, :])
+        return c
+
+    lax.fori_loop(0, 4, row_blocks(4, back_one), 0)
+    grad_copy = pltpu.make_async_copy(acc, input_grad, ls.at[9])
+    grad_copy.start()
+    rq2.r3()
     rq1.r4()
-    rv.r1()
     rq0.r5()
-    rv.r2()
-    rq2.r4()
     rv.r3()
-    rq1.r5()
-    ru1.r6()
-    ro.r6()
+
+    def result(t, c):
+        columns = pl.ds(pl.multiple_of(t * TILE, TILE), TILE)
+        u = pre[:, columns].astype(F32)
+        residual[...] += nn((u * gate(u)[0]).astype(BF), w_down[columns, :])
+        plan = {1: (rq2.r4, rv.r4), 3: (rq1.r5, ru1.r6), 5: (ro.r6, rd.r5)}
+        follow(plan, t)
+        return c
+
+    lax.fori_loop(0, 8, result, 0)
+    h2[...] = (residual[...] + vec[7:8, :]).astype(BF)
+    out_copy = pltpu.make_async_copy(h2, layer_out, ls.at[8])
+    out_copy.start()
     rq2.r5()
-    rv.r4()
+    rv.r5()
     rq0.r6()
     rq1.r6()
-    rv.r5()
     rq2.r6()
     rv.r6()
 
     for h in range(2):
         d_up[:, h * 1536 : h * 1536 + 768] = ru0.done[h]
         d_up[:, h * 1536 + 768 : h * 1536 + 1536] = ru1.done[h]
-        d_down[:, h * TILE : (h + 1) * TILE] = rd.done[h]
+        for q in range(2):
+            d_down[48 * q : 48 * q + 48, h * TILE : (h + 1) * TILE] = rd.done[h, q]
         d_out[:, h * TILE : (h + 1) * TILE] = ro.done[h]
         d_small[h] = rv.done[h]
         for k, r in enumerate((rq0, rq1, rq2)):
@@ -807,13 +1030,14 @@
         pltpu.VMEM((16, D), F32),
         pltpu.VMEM((1, FF), F32),
         pltpu.SemaphoreType.DMA((10,)),
-        pltpu.SemaphoreType.DMA((4, 16)),
-        pltpu.SemaphoreType.DMA((4, 16)),
-        pltpu.SemaphoreType.DMA((8, 17)),
-        pltpu.SemaphoreType.DMA((8, 17)),
+        pltpu.SemaphoreType.DMA((4, 23)),
+        pltpu.SemaphoreType.DMA((4, 23)),
+        pltpu.SemaphoreType.DMA((8, 25)),
+        pltpu.SemaphoreType.DMA((8, 25)),
     ]
-    for rows, half in ((24, 768), (24, 768), (96, 384), (24, 384), (24, 384), (24, 384), (24, 384), (16, SMALL)):
+    for rows, half in ((24, 768), (24, 768), (24, 384), (24, 384), (24, 384), (24, 384), (16, SMALL)):
         scratch += reduce_scratch(rows, half)
+    scratch += reduce_z_scratch(96, 384)
     shape = jax.ShapeDtypeStruct
     large = [
         shape((ROWS, D), BF),
@@ -834,7 +1058,7 @@
         out_specs=[hbm, hbm, *[vmem] * 5],
         scratch_shapes=scratch,
         compiler_params=pltpu.CompilerParams(
-            collective_id=0, has_side_effects=True, vmem_limit_bytes=63 << 20
+            collective_id=0, has_side_effects=True, vmem_limit_bytes=65400 << 10
         ),
         cost_estimate=pl.CostEstimate(flops=25 * 10**9, bytes_accessed=6 * 10**6, transcendentals=8 * 10**6),
     )(

time: 153 us -> 142 us (0.928)
  Pallas kernels: 151 us -> 141 us
    pallas_call x1, Pallas kernels: 147 us -> 136 us  [shards(): pl.pallas_call(kernel, out_shape=[*large, shape((2, 16, SMALL), F32)], in...]
where the time goes in v3:
time: 142 us
  Pallas kernels  141 us (99%)
  between operations  1.47 us (1%)
    pallas_call x1, Pallas kernels, shards(): pl.pallas_call(kernel, out_shape=[*large, shape((2, 16, SMALL), F32)], in...  136 us
    pallas_call x1, Pallas kernels, shards(): pl.pallas_call(finish, out_shape=[*large, *[shape((1, v.shape[0]), F32) f...  4.46 us

profile of v3, /device:TPU:1, one launch (start us, length us, event | category | flops | bytes accessed | tf_op | source)
XLA Modules:
  0.0 142.2 jit_solution(17784433761139007840)
XLA Ops:
  1.3 136.3 %shard_map.280 = (bf16[512,768]{1,0:T(8,128)(2,1)}, f32[512,768]{1,0:T(8,128)}, f32[24,2304]{1,0:T(8,128)}, f32[24,768]{1,0:T(8,128)}, f32[24,3072]{1,0:T(8,128)...) custom-call(bf16[512,768]{1,0:T(8,128)(2,1)} %tokens_in.1, s32[1,6]{1,0:T(1,128)} %lengths.1, s32[1,1]{1,0:T(1,128)} %bitcast.19.pads, ...), custom_call_target="tpu_custom_call" | custom-call | flops 24999999488 | bytes 6000000 | tf_op jit(solution)/shard_map/pallas_call | solution.py:1054
  137.6 4.5 %shard_map.281 = (bf16[512,768]{1,0:T(8,128)(2,1)}, f32[512,768]{1,0:T(8,128)}, f32[24,2304]{1,0:T(8,128)}, f32[24,768]{1,0:T(8,128)}, f32[24,3072]{1,0:T(8,128)...) custom-call(bf16[512,768]{1,0:T(8,128)(2,1)} %get-tuple-element.37.r, ...), custom_call_target="tpu_custom_call" | custom-call | tf_op jit(solution)/shard_map/pallas_call | solution.py:1068

commit v4 on v3

--- a/solution.py
+++ b/solution.py
@@ -342,6 +342,9 @@
 
     def add(self, place, *terms):
         here = self.s(self.w.core, *place)
+        if len(terms) == 1:
+            here[...] = here[...] + terms[0][...]
+            return
         total = here[...].astype(F32)
         for term in terms:
             total = total + term[...].astype(F32)
@@ -470,7 +473,7 @@
             def one(j, _, b=b):
                 z, a = j // 4, j % 4
                 here = self.part.at[self.w.core, b, z, a]
-                here[...] = (here[...].astype(F32) + self.tw[b, z, a].astype(F32)).astype(BF)
+                here[...] = here[...] + self.tw[b, z, a]
                 return 0
 
             lax.fori_loop(0, 8, one, 0)
@@ -557,13 +560,16 @@
     lax.fori_loop(0, 8, one, 0)
 
 
-def scatter_rows(value, part, h, first):
-    n = value.shape[1]
-    for f in range(32):
-        x, z, y = f // 8, (f // 4) % 2, f % 4
-        part[h, x + h * (y - x), z, y + h * (x - y), :, pl.ds(first, n)] = value[
-            24 * f : 24 * f + 24
-        ].astype(BF)
+def scatter_rows(left, right, part, h, first):
+    n = right.shape[1]
+    for k in range(2):
+        value = nn(left[k * TILE : (k + 1) * TILE, :], right[...])
+        for i in range(16):
+            f = 16 * k + i
+            x, z, y = f // 8, (f // 4) % 2, f % 4
+            part[h, x + h * (y - x), z, y + h * (x - y), :, pl.ds(first, n)] = value[
+                24 * i : 24 * i + 24
+            ].astype(BF)
 
 
 def stats(x):
@@ -602,9 +608,17 @@
 
 
 def gate(u):
-    square = u * u
-    th = jnp.tanh(u * (SLOPE + (SLOPE * 0.044715) * square))
-    return 0.5 + 0.5 * th, th, square
+    inner = u * (SLOPE + (SLOPE * 0.044715) * (u * u))
+    return 0.5 + 0.5 * jnp.tanh(inner), inner
+
+
+def gelu(u):
+    return u * gate(u)[0]
+
+
+def gelu_slope(u):
+    low, inner = gate(u)
+    return low + low * (1.0 - low) * (6.0 * inner - (4.0 * SLOPE) * u)
 
 
 def follow(plan, step):
@@ -632,9 +646,9 @@
 def kernel(
     tokens_in, lengths, pads, og_in, in_weight, out_weight, up_weight, down_weight,
     v0, v1, v2, v3, v4, v5, v6, v7, v8,
-    layer_out, input_grad, d_in, d_out, d_up, d_down, d_small,
+    layer_out, input_grad, s_up0, s_up1, s_out, s_in0, s_in1, s_in2, s_small, s_down,
     tokens, og, in_pack, vpack, raw_in, raw_out, raw_up, raw_down, small, w_in, w_out, w_up, w_down,
-    h1, joint, lse, attended, residual, h2, h2t, dh2, acc, pre, vec, ub, gvec, dub,
+    h1, joint, lse, attended, residual, h2, h2t, dh2, part, other, pre, vec, ub, gvec, dub,
     ls, gs, gr, rs, rr, *bufs,
 ):
     w = Where()
@@ -722,11 +736,9 @@
 
     h1[...] = (residual[...] * vec[0:1, :] + vec[1:2, :]).astype(BF)
 
-    for t in range(3):
-        bias = (vec[2:3, :], jnp.zeros((1, D), F32), vec[3:4, :])[t]
-        for u in range(2):
-            columns = slice(t * D + u * TILE, t * D + (u + 1) * TILE)
-            joint[:, columns] = (nn(h1[...], w_in[:, columns]) + bias[:, u * TILE : (u + 1) * TILE]).astype(BF)
+    for t, bias in enumerate((vec[2:3, :], 0.0, vec[3:4, :])):
+        columns = slice(t * D, (t + 1) * D)
+        joint[:, columns] = (nn(h1[...], w_in[:, columns]) + bias).astype(BF)
 
     same = codes(0)
     lane = iota((1, 128), 1)
@@ -762,11 +774,7 @@
 
     go.g4()
     assemble(raw_out, w_out, TILE)
-    for u in range(2):
-        columns = slice(u * TILE, (u + 1) * TILE)
-        residual[:, columns] = (
-            tokens[:, columns].astype(F32) + nn(attended[...], w_out[:, columns]) + vec[4:5, columns]
-        )
+    residual[...] = tokens[...].astype(F32) + nn(attended[...], w_out[...]) + vec[4:5, :]
 
     def norm_two(rows, c):
         normed, _ = stats(residual[rows, :])
@@ -777,6 +785,15 @@
     h2t[...] = h2[...].T
     gu.g4()
     assemble(raw_up, w_up, 1536)
+    def wide(t):
+        return pl.ds(pl.multiple_of(t * D, D), D)
+
+    def ahead(t, c):
+        columns = wide(t)
+        pre[:, columns] = (nn(h2[...], w_up[:, columns]) + ub[:, columns]).astype(BF)
+        return c
+
+    lax.fori_loop(0, 4, ahead, 0)
     gd.g3z()
     gd.g4()
     assemble(raw_down, w_down, TILE)
@@ -784,53 +801,62 @@
         g.end()
 
 
-    def forth(t, c):
-        columns = pl.ds(pl.multiple_of(t * TILE, TILE), TILE)
-        u = nn(h2[...], w_up[:, columns]) + ub[:, columns]
-        pre[:, columns] = u.astype(BF)
-        act = (u * gate(u)[0]).astype(BF)
-        grad_down = tn(act, og[...]).astype(BF)
-        x, z = t // 2, t % 2
-        for y in range(4):
-            raw_down[0, x, z, y] = grad_down[96 * y : 96 * y + 96, :TILE]
-            raw_down[1, y, z, x] = grad_down[96 * y : 96 * y + 96, TILE:]
+    def activate(to, t):
+        to[...] = gelu(pre[:, wide(t)].astype(F32)).astype(BF)
+
+    def forth(i, c):
+        for now, later, t in ((part, other, 2 * i), (other, part, 2 * i + 1)):
+            activate(later, (t + 1) % 4)
+            grad = tn(now[...], og[...])
+            for f in range(8):
+                z, y, rows = f // 4, f % 4, slice(96 * f, 96 * f + 96)
+                raw_down[0, t, z, y] = grad[rows, :TILE].astype(BF)
+                raw_down[1, y, z, t] = grad[rows, TILE:].astype(BF)
         return c
 
-    lax.fori_loop(0, 8, forth, 0)
+    activate(part, 0)
+    lax.fori_loop(0, 2, forth, 0)
     rd.r0()
+
     dh2[...] = jnp.zeros_like(dh2)
 
-    def back(i, c):
-        t = i // 2 + 4 * (i % 2)
-        columns = pl.ds(pl.multiple_of(t * TILE, TILE), TILE)
-        u = pre[:, columns].astype(F32)
-        low, th, square = gate(u)
-        slope = low + u * (1.0 - th * th) * (0.5 * SLOPE + (1.5 * 0.044715 * SLOPE) * square)
-        grad_pre = (nt(og[...], w_down[columns, :]) * slope).astype(BF)
-        dub[:, columns] = column_sum(grad_pre.astype(F32))
-        scatter_rows(nn(h2t[...], grad_pre), raw_up, t // 4, pl.multiple_of((t % 4) * TILE, 128))
-        dh2[...] += nt(grad_pre, w_up[:, columns])
-        plan = {
-            1: (only(rd.r1, 0),),
-            2: (only(rd.r1, 1),),
-            3: (ru0.r0, only(rd.r1, 2)),
-            4: (only(rd.r1, 3),),
-            6: (ru0.r1,),
-        }
-        follow(plan, i)
+    def tile_at(i):
+        return i // 2 + 2 * (i % 2)
+
+    def front(to, t):
+        columns = wide(t)
+        total = jnp.zeros((1, D), F32)
+        for r in range(0, ROWS, 256):
+            slope = gelu_slope(pre[r : r + 256, columns].astype(F32))
+            grad_pre = (nt(og[r : r + 256, :], w_down[columns, :]) * slope).astype(BF)
+            to[r : r + 256, :] = grad_pre
+            total = total + column_sum(grad_pre.astype(F32))
+        dub[:, columns] = total
+
+    def back(j, c):
+        for now, later, i in ((part, other, 2 * j), (other, part, 2 * j + 1)):
+            t = tile_at(i)
+            front(later, tile_at((i + 1) % 4))
+            scatter_rows(h2t, now, raw_up, t // 2, pl.multiple_of((t % 2) * D, 128))
+            dh2[...] += nt(now[...], w_up[:, wide(t)])
+            plan = {
+                0: (only(rd.r1, 0),),
+                1: (ru0.r0, only(rd.r1, 1), only(rd.r1, 2)),
+                2: (only(rd.r1, 3),),
+                3: (ru0.r1,),
+            }
+            follow(plan, i)
         return c
 
-    lax.fori_loop(0, 8, back, 0)
+    front(part, 0)
+    lax.fori_loop(0, 2, back, 0)
     ru1.r0()
-    rd.r2((0,))
-    ru0.r2()
 
     def back_two(rows, c):
         normed, inv = stats(residual[rows, :])
         grad = dh2[rows, :]
         up = og[rows, :].astype(F32)
         total = up + norm_backward(grad, normed, inv, vec[5:6, :])
-        acc[rows, :] = total
         rounded = total.astype(BF)
         w_up[rows, 0:D] = rounded
         return (
@@ -844,16 +870,17 @@
     sums = lax.fori_loop(0, 4, row_blocks(4, back_two), (zero, zero, zero, zero))
     for j, v in zip((4, 5, 6, 7), sums):
         gvec[j : j + 1, :] = v
-    ru1.r1()
     grad_branch = w_up.at[0:ROWS, 0:D]
     grad_attended = w_up.at[0:ROWS, D : 2 * D]
+    attended_t = h2t
+    attended_t[...] = attended[...].T
     for u in range(2):
         columns = slice(u * TILE, (u + 1) * TILE)
-        scatter_rows(tn(attended[...], grad_branch[:, columns]), raw_out, u, 0)
-        grad_attended[:, columns] = nt(grad_branch[...], w_out[columns, :]).astype(BF)
+        scatter_rows(attended_t, grad_branch.at[:, columns], raw_out, u, 0)
+    grad_attended[...] = nt(grad_branch[...], w_out[...]).astype(BF)
     ro.r0()
-    rd.r2((1,))
-    ru0.r3()
+    ru0.r2()
+    ru1.r1()
     h1t = h2t
     h1t[...] = h1[...].T
 
@@ -880,15 +907,16 @@
         joint[:, cq], joint[:, ck], joint[:, cv] = dq, dk, dv
         gvec[2:3, cq] = column_sum(dq.astype(F32))
         gvec[3:4, cq] = column_sum(dv.astype(F32))
-        both = jnp.concatenate([dq, dk, dv], axis=1)
-        scatter_rows(nn(h1t[...], both), raw_in, p % 2, pl.multiple_of((p // 2) * TILE, 128))
+        both = part.at[:, 0:TILE]
+        both[:, 0:128], both[:, 128:256], both[:, 256:384] = dq, dk, dv
+        scatter_rows(h1t, both, raw_in, p % 2, pl.multiple_of((p // 2) * TILE, 128))
         plan = (
-            (ro.r1, ru1.r2),
-            (rq0.r0, ru0.r4, only(rd.r2, 2)),
-            (rq0.r1, ro.r2, ru1.r3, ru0.r5),
-            (rq1.r0, rq0.r2, ro.r3, ru1.r4, only(rd.r2, 3)),
-            (rq1.r1, rq0.r3, ro.r4, ru0.r6),
-            (rq2.r0, rd.r3, rq1.r2, ru1.r5, rq0.r4),
+            (ro.r1,),
+            (rq0.r0, ru0.r3, ru1.r2),
+            (rq0.r1, ro.r2, ru0.r4),
+            (rq1.r0, rq0.r2, ru1.r3, ro.r3),
+            (rq1.r1, ru0.r5, rd.r2, ru1.r4),
+            (rq2.r0, rq0.r3, rq1.r2, ro.r4, rd.r3),
         )
         follow(dict(enumerate(plan)), p)
         return c
@@ -896,9 +924,7 @@
     lax.fori_loop(0, 6, attend_back, 0)
 
     rq2.r1()
-    for u in range(2):
-        columns = slice(u * TILE, (u + 1) * TILE)
-        dh2[:, columns] = nt(joint[...], w_in[columns, :])
+    dh2[...] = nt(joint[...], w_in[...])
 
     def sums_one(rows, c):
         normed, _ = stats(tokens[rows, :].astype(F32))
@@ -922,70 +948,81 @@
     rv.r0()
     rq2.r2()
     rd.r4()
+    rq0.r4()
     rq1.r3()
+    ru1.r5()
     ro.r5()
     rv.r1()
     rv.r2()
 
     def back_one(rows, c):
         normed, inv = stats(tokens[rows, :].astype(F32))
-        acc[rows, :] = acc[rows, :] + norm_backward(dh2[rows, :], normed, inv, vec[0:1, :])
+        dh2[rows, :] = grad_branch[rows, :].astype(F32) + norm_backward(dh2[rows, :], normed, inv, vec[0:1, :])
         return c
 
     lax.fori_loop(0, 4, row_blocks(4, back_one), 0)
-    grad_copy = pltpu.make_async_copy(acc, input_grad, ls.at[9])
+    grad_copy = pltpu.make_async_copy(dh2, input_grad, ls.at[9])
     grad_copy.start()
     rq2.r3()
     rq1.r4()
     rq0.r5()
     rv.r3()
+    for t in range(4):
+        activate(pre.at[:, t * D : (t + 1) * D], t)
+    rq2.r4()
+    rv.r4()
 
     def result(t, c):
-        columns = pl.ds(pl.multiple_of(t * TILE, TILE), TILE)
-        u = pre[:, columns].astype(F32)
-        residual[...] += nn((u * gate(u)[0]).astype(BF), w_down[columns, :])
-        plan = {1: (rq2.r4, rv.r4), 3: (rq1.r5, ru1.r6), 5: (ro.r6, rd.r5)}
-        follow(plan, t)
+        columns = pl.ds(pl.multiple_of(t * 256, 256), 256)
+        h2[:, columns] = (residual[:, columns] + vec[7:8, columns] + nn(pre[...], w_down[:, columns])).astype(BF)
+        follow({1: (rq2.r5, rq1.r5, rv.r5)}, t)
         return c
 
-    lax.fori_loop(0, 8, result, 0)
-    h2[...] = (residual[...] + vec[7:8, :]).astype(BF)
+    lax.fori_loop(0, 3, result, 0)
     out_copy = pltpu.make_async_copy(h2, layer_out, ls.at[8])
     out_copy.start()
-    rq2.r5()
-    rv.r5()
-    rq0.r6()
-    rq1.r6()
-    rq2.r6()
-    rv.r6()
-
-    for h in range(2):
-        d_up[:, h * 1536 : h * 1536 + 768] = ru0.done[h]
-        d_up[:, h * 1536 + 768 : h * 1536 + 1536] = ru1.done[h]
-        for q in range(2):
-            d_down[48 * q : 48 * q + 48, h * TILE : (h + 1) * TILE] = rd.done[h, q]
-        d_out[:, h * TILE : (h + 1) * TILE] = ro.done[h]
-        d_small[h] = rv.done[h]
-        for k, r in enumerate((rq0, rq1, rq2)):
-            for j in range(3):
-                to = j * D + (2 * k + h) * 128
-                d_in[:, to : to + 128] = r.done[h, :, 128 * j : 128 * j + 128]
-    for r in (ru0, ru1, rd, ro, rq0, rq1, rq2, rv):
+    sums = (ru0, ru1, ro, rq0, rq1, rq2, rv, rd)
+    hand = [
+        pltpu.make_async_copy(r.done, to, ls.at[10 + i])
+        for i, (r, to) in enumerate(
+            zip(sums, (s_up0, s_up1, s_out, s_in0, s_in1, s_in2, s_small, s_down))
+        )
+    ]
+    for r, c in zip(sums, hand):
+        (r.r5 if r is rd else r.r6)()
+        c.start()
+
+    for r in sums:
         r.end()
     out_copy.wait()
     grad_copy.wait()
-
-
-def finish(*refs):
-    packed, src, dst, vectors = refs[6], refs[:6], refs[7:13], refs[13:22]
-    held, taken, given = refs[22:28], refs[28], refs[29]
-    arrive = [pltpu.make_async_copy(s, h, taken.at[i]) for i, (s, h) in enumerate(zip(src, held))]
-    leave = [pltpu.make_async_copy(h, d, given.at[i]) for i, (h, d) in enumerate(zip(held, dst))]
+    for c in hand:
+        c.wait()
+
+
+def finish(
+    layer_in, grad_in, up0, up1, out, in0, in1, in2, small, down,
+    layer_out, grad_out, d_in, d_out, d_up, d_down, v0, v1, v2, v3, v4, v5, v6, v7, v8,
+    held_layer, held_grad, taken, given,
+):
+    pairs = ((layer_in, held_layer, layer_out), (grad_in, held_grad, grad_out))
+    arrive = [pltpu.make_async_copy(s, h, taken.at[i]) for i, (s, h, d) in enumerate(pairs)]
+    leave = [pltpu.make_async_copy(h, d, given.at[i]) for i, (s, h, d) in enumerate(pairs)]
     for c in arrive:
         c.start()
-    for j in range(8):
-        vectors[j][...] = packed[0, j : j + 1, 0:24]
-    vectors[8][...] = packed[1, 0:1, 0:96]
+    for h in range(2):
+        d_up[:, h * 1536 : h * 1536 + 768] = up0[h]
+        d_up[:, h * 1536 + 768 : h * 1536 + 1536] = up1[h]
+        for q in range(2):
+            d_down[48 * q : 48 * q + 48, h * TILE : (h + 1) * TILE] = down[h, q]
+        d_out[:, h * TILE : (h + 1) * TILE] = out[h]
+        for k, part in enumerate((in0, in1, in2)):
+            for j in range(3):
+                to = j * D + (2 * k + h) * 128
+                d_in[:, to : to + 128] = part[h, :, 128 * j : 128 * j + 128]
+    for j, v in enumerate((v0, v1, v2, v3, v4, v5, v6, v7)):
+        v[...] = small[0, j : j + 1, 0:24]
+    v8[...] = small[1, 0:1, 0:96]
     for c, d in zip(arrive, leave):
         c.wait()
         d.start()
@@ -1023,13 +1060,14 @@
         pltpu.VMEM((ROWS, D), BF),
         pltpu.VMEM((D, ROWS), BF),
         pltpu.VMEM((ROWS, D), F32),
-        pltpu.VMEM((ROWS, D), F32),
+        pltpu.VMEM((ROWS, D), BF),
+        pltpu.VMEM((ROWS, D), BF),
         pltpu.VMEM((ROWS, FF), BF),
         pltpu.VMEM((16, D), F32),
         pltpu.VMEM((1, FF), F32),
         pltpu.VMEM((16, D), F32),
         pltpu.VMEM((1, FF), F32),
-        pltpu.SemaphoreType.DMA((10,)),
+        pltpu.SemaphoreType.DMA((18,)),
         pltpu.SemaphoreType.DMA((4, 23)),
         pltpu.SemaphoreType.DMA((4, 23)),
         pltpu.SemaphoreType.DMA((8, 25)),
@@ -1051,11 +1089,13 @@
         first_gain, first_shift, query_bias, value_bias, output_bias, second_gain, second_shift, down_bias,
         up_bias,
     )
+    halves = [shape((2, 24, 768), F32)] * 2 + [shape((2, 24, 384), F32)] * 4
+    halves += [shape((2, 16, SMALL), F32), shape((2, 2, 48, 384), F32)]
     results = pl.pallas_call(
         kernel,
-        out_shape=[*large, shape((2, 16, SMALL), F32)],
+        out_shape=[*large[:2], *halves],
         in_specs=[hbm, smem, smem, hbm, hbm, hbm, hbm, hbm, *[vmem] * 9],
-        out_specs=[hbm, hbm, *[vmem] * 5],
+        out_specs=[hbm] * 10,
         scratch_shapes=scratch,
         compiler_params=pltpu.CompilerParams(
             collective_id=0, has_side_effects=True, vmem_limit_bytes=65400 << 10
@@ -1068,12 +1108,12 @@
     done = pl.pallas_call(
         finish,
         out_shape=[*large, *[shape((1, v.shape[0]), F32) for v in vectors]],
-        in_specs=[*[hbm] * 6, vmem],
-        out_specs=[*[hbm] * 6, *[vmem] * 9],
+        in_specs=[hbm, hbm, *[vmem] * 8],
+        out_specs=[hbm, hbm, *[vmem] * 13],
         scratch_shapes=[
-            *[pltpu.VMEM(x.shape, x.dtype) for x in large],
-            pltpu.SemaphoreType.DMA((6,)),
-            pltpu.SemaphoreType.DMA((6,)),
+            *[pltpu.VMEM(x.shape, x.dtype) for x in large[:2]],
+            pltpu.SemaphoreType.DMA((2,)),
+            pltpu.SemaphoreType.DMA((2,)),
         ],
     )(*results)
     layer_out, input_grad, d_in, d_out, d_up, d_down = done[:6]

time: 142 us -> 139 us (0.979)
  Pallas kernels: 141 us -> 137 us
    pallas_call x1, Pallas kernels: 136 us -> 132 us  [shards(): pl.pallas_call(kernel, out_shape=[*large[:2], *halves], in_specs=[hbm, sm...]
where the time goes in v4:
time: 139 us
  Pallas kernels  137 us (99%)
  between operations  1.49 us (1%)
    pallas_call x1, Pallas kernels, shards(): pl.pallas_call(kernel, out_shape=[*large[:2], *halves], in_specs=[hbm, sm...  132 us
    pallas_call x1, Pallas kernels, shards(): pl.pallas_call(finish, out_shape=[*large, *[shape((1, v.shape[0]), F32) f...  5.02 us

profile of v4, /device:TPU:1, one launch (start us, length us, event | category | flops | bytes accessed | tf_op | source)
XLA Modules:
  0.0 138.6 jit_solution(11910791299925990744)
XLA Ops:
  1.3 132.1 %shard_map.280 = (bf16[512,768]{1,0:T(8,128)(2,1)}, f32[512,768]{1,0:T(8,128)}, f32[2,24,768]{2,1,0:T(8,128)}, f32[2,24,768]{2,1,0:T(8,128)}, f32[2,24,384]{2,1,...) custom-call(bf16[512,768]{1,0:T(8,128)(2,1)} %tokens_in.1, ...), custom_call_target="tpu_custom_call" | custom-call | flops 24999999488 | bytes 6000000 | tf_op jit(solution)/shard_map/pallas_call | solution.py:1094
  133.4 5.0 %shard_map.281 = (bf16[512,768]{1,0:T(8,128)(2,1)}, f32[512,768]{1,0:T(8,128)}, f32[24,2304]{1,0:T(8,128)}, f32[24,768]{1,0:T(8,128)}, f32[24,3072]{1,0:T(8,128)...) custom-call(bf16[512,768]{1,0:T(8,128)(2,1)} %get-tuple-element.40.l, ...), custom_call_target="tpu_custom_call" | custom-call | tf_op jit(solution)/shard_map/pallas_call | solution.py:1108

commit v5 on v4

--- a/solution.py
+++ b/solution.py
@@ -47,7 +47,6 @@
         self.z = self.zh * 2 + self.zl
         self.twin = {"rep": self.r + 1 - 2 * c, "fsdp": self.f}
         self.pair = {"rep": (1 - self.zl) * 2 + c, "fsdp": self.f}
-        self.diagonal = {"rep": (1 - self.zl) * 2 + 1 - c, "fsdp": self.f}
         self.cross, self.cross_up, self.cross_down, self.cross_far = [self.over(i) for i in (0, 1, 3, 2)]
         self.third = {"rep": self.r, "fsdp": (self.x * 2 + self.zo) * 4 + self.y}
 
@@ -65,7 +64,7 @@
 
     def friends(self):
         near = [self.a_up, self.a_down, self.a_far, self.b_up, self.b_down, self.b_far, self.twin]
-        return near + [self.pair, self.diagonal, self.third, self.cross, self.cross_up, self.cross_down, self.cross_far]
+        return near + [self.pair, self.third, self.cross, self.cross_up, self.cross_down, self.cross_far]
 
     def greet(self):
         sem = pltpu.get_barrier_semaphore()
@@ -104,16 +103,22 @@
 class Gather(Copies):
     count = 16
 
-    def __init__(self, w, src, raw, direct, local, ss, rs):
+    def __init__(self, w, src, raw, direct, window, local, ss, rs):
         self.w, self.src, self.raw, self.direct, self.ss, self.rs = w, src, raw, direct, ss, rs
         self.half = src.shape[1] // 2
+        self.first, self.width = window or (0, self.half)
         self.local = pltpu.make_async_copy(self.own(), self.slot(w.b, w.zh, w.a), local)
 
     def own(self):
-        return self.src.at[:, pl.ds(pl.multiple_of(self.w.core * self.half, 128), self.half)]
+        start = self.w.core * self.half + self.first
+        return self.src.at[:, pl.ds(pl.multiple_of(start, 128), self.width)]
 
     def slot(self, *i):
-        return self.raw.at[(self.w.core, *i)]
+        return self.place(self.w.core, *i)
+
+    def place(self, *i):
+        left = (slice(None),) * (5 - len(i))
+        return self.raw.at[(*i, *left, pl.ds(self.first, self.width))]
 
     def route(self, k):
         w = self.w
@@ -147,15 +152,15 @@
             return self.slot(w.b, w.zh if k < 3 else w.zo, (w.am, w.ap, w.a2, w.a, w.am, w.ap, w.a2)[k])
         if k >= 11:
             o = 1 - w.core
-            return self.raw.at[
-                {
+            return self.place(
+                *{
                     11: (o, w.a),
                     12: (o, w.am),
                     13: (o, w.ap),
                     14: (o, w.a2, 0),
                     15: (o, w.a2, 1),
                 }[k]
-            ]
+            )
         return self.slot(*{7: (w.bm,), 8: (w.bp,), 9: (w.b2, 0), 10: (w.b2, 1)}[k])
 
     def g0(self):
@@ -413,127 +418,6 @@
         self.take(16)
 
 
-class ReduceZ(Copies):
-    def __init__(self, w, part, bufs, ss, rs):
-        self.w, self.part, self.ss, self.rs = w, part, ss, rs
-        self.tw, self.zr, self.fx, self.af, self.done = bufs
-        self.half = self.af.shape[-2]
-        self.rows = (w.b2, w.bp, w.bm, w.b)
-        self.count = 25
-
-    def s(self, b, z, a, q):
-        return self.part.at[
-            self.w.core, b, z, a, pl.ds(pl.multiple_of(q * self.half, 16), self.half), :
-        ]
-
-    def route(self, k):
-        w, c, every = self.w, self.w.core, slice(None)
-        if k < 4:
-            j = (w.a2, w.ap, w.am, w.a)[k]
-            return self.part.at[1 - c, j], self.tw.at[j], w.twin
-        if k < 16:
-            b, d = self.rows[(k - 4) // 3], (k - 4) % 3
-            z, q, device = (
-                (w.zh, 1 - w.zl, w.pair),
-                (w.zo, 1 - w.zl, w.cross),
-                (w.zo, w.zl, w.third),
-            )[d]
-            return self.s(b, z, every, q), self.zr.at[d, b], device
-        if k >= 22:
-            here = self.done.at[c, w.zl]
-            return here, here, (w.twin, w.pair, w.diagonal)[k - 22]
-        b, a, device = {
-            16: (w.b2, every, w.b_far),
-            17: (w.bp, every, w.b_up),
-            18: (w.bm, every, w.b_down),
-            19: (w.b, w.a2, w.a_far),
-            20: (w.b, w.ap, w.a_up),
-            21: (w.b, w.am, w.a_down),
-        }[k]
-        return self.s(b, w.zh, a, w.zl), self.lands(k), device
-
-    def lands(self, k):
-        w, c = self.w, self.w.core
-        if k < 4:
-            return self.tw.at[self.rows[k]]
-        if k < 16:
-            return self.zr.at[(k - 4) % 3, self.rows[(k - 4) // 3]]
-        if k < 22:
-            return (self.fx if k < 19 else self.af).at[(2, 0, 1)[(k - 16) % 3]]
-        return self.done.at[((1 - c, w.zl), (c, 1 - w.zl), (1 - c, 1 - w.zl))[k - 22]]
-
-    def r0(self):
-        self.send(0, 1, 2, 3)
-
-    def r1(self, which=(0, 1, 2, 3)):
-        for i in which:
-            b = self.rows[i]
-            self.take(i)
-
-            def one(j, _, b=b):
-                z, a = j // 4, j % 4
-                here = self.part.at[self.w.core, b, z, a]
-                here[...] = here[...] + self.tw[b, z, a]
-                return 0
-
-            lax.fori_loop(0, 8, one, 0)
-            self.send(6 + 3 * i, 4 + 3 * i, 5 + 3 * i)
-
-    def r2(self, which=(0, 1, 2, 3)):
-        w = self.w
-        for i in which:
-            b = self.rows[i]
-            self.take(4 + 3 * i, 5 + 3 * i, 6 + 3 * i)
-
-            def one(a, _, b=b):
-                self.sum_up(self.s(b, w.zh, a, w.zl), *[self.zr.at[d, b, a] for d in range(3)])
-                return 0
-
-            lax.fori_loop(0, 4, one, 0)
-            if i < 3:
-                self.send(16 + i)
-
-    def sum_up(self, here, *terms):
-        total = here[...].astype(F32)
-        for term in terms:
-            total = total + term[...].astype(F32)
-        here[...] = total.astype(BF)
-
-    def r3(self):
-        w = self.w
-        self.take(16, 17, 18)
-
-        def one(a, _):
-            self.sum_up(self.s(w.b, w.zh, a, w.zl), *[self.fx.at[d, a] for d in range(3)])
-            return 0
-
-        lax.fori_loop(0, 4, one, 0)
-        self.send(19, 20, 21)
-
-    def r4(self):
-        w = self.w
-        self.take(19, 20, 21)
-        total = self.s(w.b, w.zh, w.a, w.zl)[...].astype(F32)
-        for d in range(3):
-            total = total + self.af[d].astype(F32)
-        self.done[w.core, w.zl] = total
-        self.send(22, 23, 24)
-
-    def r5(self):
-        self.take(22, 23, 24)
-
-
-def reduce_z_scratch(rows, half):
-    part = rows // 2
-    return [
-        pltpu.VMEM((4, 2, 4, rows, half), BF),
-        pltpu.VMEM((3, 4, 4, part, half), BF),
-        pltpu.VMEM((3, 4, part, half), BF),
-        pltpu.VMEM((3, part, half), BF),
-        pltpu.VMEM((2, 2, part, half), F32),
-    ]
-
-
 def reduce_scratch(rows, half):
     return [
         pltpu.VMEM((4, 2, 4, rows, half), BF),
@@ -544,7 +428,7 @@
     ]
 
 
-def assemble(raw, out, width):
+def assemble(raw, out, width, source=0, target=0):
     rows = raw.shape[4]
 
     def one(g, _):
@@ -552,9 +436,13 @@
         place = pl.ds(pl.multiple_of(g * 4 * rows, 4 * rows), 4 * rows)
         for h in range(2):
             parts = [
-                raw[0, x, z, y, :, :width] if h == 0 else raw[1, y, z, x, :, :width] for y in range(4)
+                raw[0, x, z, y, :, source : source + width]
+                if h == 0
+                else raw[1, y, z, x, :, source : source + width]
+                for y in range(4)
             ]
-            out[place, h * width : (h + 1) * width] = jnp.concatenate(parts, axis=0)
+            to = target + h * width
+            out[place, to : to + width] = jnp.concatenate(parts, axis=0)
         return 0
 
     lax.fori_loop(0, 8, one, 0)
@@ -630,10 +518,6 @@
                 stage()
 
 
-def only(stage, i):
-    return lambda: stage((i,))
-
-
 def row_blocks(count, body):
     step = ROWS // count
 
@@ -653,38 +537,38 @@
 ):
     w = Where()
     w.greet()
-    loads = [
-        pltpu.make_async_copy(src, dst, ls.at[i])
-        for i, (src, dst) in enumerate(
+    pack = ((0, 0, 256), (768, 256, 128), (256, 512, 512), (1024, 1024, 256))
+    pack += ((896, 1280, 128), (1536, 1408, 256), (1280, 1792, 256), (1792, 2048, 512))
+    moves = [(in_weight.at[:, a : a + n], in_pack.at[:, b : b + n]) for a, b, n in pack]
+    moves += [(tokens_in, tokens), (og_in, og)]
+    loads = [pltpu.make_async_copy(src, dst, ls.at[18 + i]) for i, (src, dst) in enumerate(moves)]
+    for load in loads:
+        load.start()
+    ga, gb, go, gu = [
+        Gather(w, s, r, i < 2, window, ls.at[(4, 28, 5, 6)[i]], gs.at[i], gr.at[i])
+        for i, (s, r, window) in enumerate(
             (
-                (in_weight.at[:, 0:1152], in_pack.at[:, 0:1152]),
-                (in_weight.at[:, 1152:2304], in_pack.at[:, 1280:2432]),
-                (tokens_in, tokens),
-                (og_in, og),
+                (in_pack, raw_in, (0, 512)),
+                (in_pack, raw_in, (512, 768)),
+                (out_weight, raw_out, None),
+                (up_weight, raw_up, None),
             )
         )
     ]
-    for load in loads:
-        load.start()
-    gq, go, gu = [
-        Gather(w, s, r, i == 0, ls.at[4 + i], gs.at[i], gr.at[i])
-        for i, (s, r) in enumerate(((in_pack, raw_in), (out_weight, raw_out), (up_weight, raw_up)))
-    ]
-    gd = GatherZ(w, down_weight, raw_down, ls.at[7], gs.at[3], gr.at[3])
-    every = (gq, go, gu, gd)
+    gd = GatherZ(w, down_weight, raw_down, ls.at[7], gs.at[4], gr.at[4])
+    every = (ga, gb, go, gu, gd)
     places = [(raw_up, 0, False), (raw_up, 768, False), (raw_out, 0, False)]
-    places += [(raw_in, 0, False), (raw_in, 384, False), (raw_in, 768, True), (small, 0, True)]
-    ru0, ru1, ro, rq0, rq1, rq2, rv = [
+    places += [(raw_in, 0, False), (raw_in, 384, False), (raw_in, 768, True), (small, 0, True), (raw_down, 0, False)]
+    ru0, ru1, ro, rq0, rq1, rq2, rv, rd = [
         Reduce(w, part, first, direct, bufs[5 * i : 5 * i + 5], rs.at[i], rr.at[i])
         for i, (part, first, direct) in enumerate(places)
     ]
-    rd = ReduceZ(w, raw_down, bufs[35:40], rs.at[7], rr.at[7])
     vpack[...] = jnp.zeros_like(vpack)
     for j, v in enumerate((v0, v1, v2, v3, v4, v5, v6, v7)):
         vpack[j : j + 1, 0:24] = v[...].astype(F32)
     vpack[8:9, 0:96] = v8[...].astype(F32)
-    in_pack[:, 1152:1280] = vpack[...].astype(BF)
-    in_pack[:, 2432:2560] = jnp.zeros((24, SMALL), BF)
+    in_pack[:, 384:512] = vpack[...].astype(BF)
+    in_pack[:, 1664:1792] = jnp.zeros((24, SMALL), BF)
     gvec[...] = jnp.zeros_like(gvec)
 
     def codes(dim):
@@ -696,49 +580,55 @@
             start = start + lengths[0, j]
         return jnp.where(pos < ROWS - pads[0, 0], seg, -1 - pos)
 
-    loads[0].wait()
-    loads[1].wait()
+    for load in loads[:8]:
+        load.wait()
     w.meet()
     for g in every:
         g.g0()
 
-    loads[2].wait()
-    loads[3].wait()
+    loads[8].wait()
+    loads[9].wait()
 
     def norm_one(rows, c):
         residual[rows, :] = stats(tokens[rows, :].astype(F32))[0]
         return c
 
     lax.fori_loop(0, 4, row_blocks(4, norm_one), 0)
+    ga.g1()
     go.g0a()
     gu.g0a()
-    gq.g1()
+    gb.g1()
+    ga.g2()
     go.g0b()
     gu.g0b()
     gd.g1()
+    ga.g3()
+    gb.g2()
     go.g1()
-    gq.g2()
     gu.g1()
     gd.g2()
-    gq.g3()
-    gq.g4()
-    assemble(raw_in, w_in, 1152)
-
-    packed = raw_in[0, :, :, :, 0:16, 1152:1280].reshape(32 * 16, SMALL)
+    ga.g4()
+    assemble(raw_in, w_in, TILE, 0, 0)
+
+    packed = raw_in[0, :, :, :, 0:16, 384:512].reshape(32 * 16, SMALL)
     spread = nn(packed, select24())
     n, row = iota((ROWS, D), 1), iota((ROWS, D), 0)
     spread = jnp.where(by24(n) == lax.shift_right_logical(row, 4), spread, 0.0)
     vec[...] = jnp.sum(spread.reshape(32, 16, D), axis=0)
-    packed = raw_in[0, :, :, :, 0:16, 1152:1280].reshape(32, 16, SMALL)[:, 8:9].reshape(32, SMALL)
+    packed = raw_in[0, :, :, :, 0:16, 384:512].reshape(32, 16, SMALL)[:, 8:9].reshape(32, SMALL)
     spread = nn(packed, select96())
     n, row = iota((32, FF), 1), iota((32, FF), 0)
     ub[...] = column_sum(jnp.where(lax.shift_right_logical(by24(n), 2) == row, spread, 0.0))
 
     h1[...] = (residual[...] * vec[0:1, :] + vec[1:2, :]).astype(BF)
 
-    for t, bias in enumerate((vec[2:3, :], 0.0, vec[3:4, :])):
-        columns = slice(t * D, (t + 1) * D)
-        joint[:, columns] = (nn(h1[...], w_in[:, columns]) + bias).astype(BF)
+    def project(first, heads, at):
+        n = heads * HEAD
+        for t, bias in enumerate((vec[2:3, at : at + n], 0.0, vec[3:4, at : at + n])):
+            columns = slice(first + t * n, first + (t + 1) * n)
+            joint[:, columns] = (nn(h1[...], w_in[:, columns]) + bias).astype(BF)
+
+    project(0, 4, 0)
 
     same = codes(0)
     lane = iota((1, 128), 1)
@@ -749,7 +639,12 @@
         return jnp.where(same == codes(1), nt(keys, picked), LOW)
 
     def pair_columns(p):
-        return [pl.ds(pl.multiple_of(t * D + p * 128, 128), 128) for t in range(3)]
+        late = (p + 4) // 6
+        start = p * 128 + late * 512
+        return [pl.ds(pl.multiple_of(start + t * (256 + 256 * late), 128), 128) for t in range(3)]
+
+    def pair_lanes(p):
+        return pl.ds(pl.multiple_of(p * 128, 128), 128)
 
     def attend(p, c):
         cq, ck, cv = pair_columns(p)
@@ -764,13 +659,17 @@
             lse[2 * p + first] = top + jnp.log(total)
             o = tn(weights, values)
             mixed = o if first == 0 else jnp.where(lane < 64, mixed, o)
-        attended[:, cq] = mixed.astype(BF)
-
-        plan = ((gd.g3,), (go.g2,), (gu.g2,), (go.g3,), (), (gu.g3,))
+        attended[:, pair_lanes(p)] = mixed.astype(BF)
+
+        plan = ((gb.g3, go.g2), (gu.g2,), (gd.g3,), (go.g3, gu.g3), (), (gd.g3z,))
         follow(dict(enumerate(plan)), p)
         return c
 
-    lax.fori_loop(0, 6, attend, 0)
+    lax.fori_loop(0, 2, attend, 0)
+    gb.g4()
+    assemble(raw_in, w_in, D, 512, D)
+    project(D, 8, 256)
+    lax.fori_loop(2, 6, attend, 0)
 
     go.g4()
     assemble(raw_out, w_out, TILE)
@@ -794,7 +693,6 @@
         return c
 
     lax.fori_loop(0, 4, ahead, 0)
-    gd.g3z()
     gd.g4()
     assemble(raw_down, w_down, TILE)
     for g in every:
@@ -840,10 +738,8 @@
             scatter_rows(h2t, now, raw_up, t // 2, pl.multiple_of((t % 2) * D, 128))
             dh2[...] += nt(now[...], w_up[:, wide(t)])
             plan = {
-                0: (only(rd.r1, 0),),
-                1: (ru0.r0, only(rd.r1, 1), only(rd.r1, 2)),
-                2: (only(rd.r1, 3),),
-                3: (ru0.r1,),
+                1: (ru0.r0, rd.r1),
+                3: (ru0.r1, rd.r2),
             }
             follow(plan, i)
         return c
@@ -879,15 +775,18 @@
         scatter_rows(attended_t, grad_branch.at[:, columns], raw_out, u, 0)
     grad_attended[...] = nt(grad_branch[...], w_out[...]).astype(BF)
     ro.r0()
-    ru0.r2()
     ru1.r1()
     h1t = h2t
     h1t[...] = h1[...].T
 
-    def attend_back(p, c):
+    def weight_gradient(p, both):
+        scatter_rows(h1t, both.at[:, 0:TILE], raw_in, p % 2, pl.multiple_of((p // 2) * TILE, 128))
+
+    def pair_back(p, both):
         cq, ck, cv = pair_columns(p)
         queries, keys, values = joint[:, cq], joint[:, ck], joint[:, cv]
-        gradient = grad_attended[:, cq]
+        lanes = pair_lanes(p)
+        gradient = grad_attended[:, lanes]
         dq = dk = dv = None
         for first in range(2):
             mine = (lane >= 64 * first) & (lane < 64 * first + 64)
@@ -905,23 +804,29 @@
                 dq, dk, dv = [jnp.where(lane < 64, l, r) for l, r in ((dq, q), (dk, k), (dv, v))]
         dq, dk, dv = dq.astype(BF), dk.astype(BF), dv.astype(BF)
         joint[:, cq], joint[:, ck], joint[:, cv] = dq, dk, dv
-        gvec[2:3, cq] = column_sum(dq.astype(F32))
-        gvec[3:4, cq] = column_sum(dv.astype(F32))
-        both = part.at[:, 0:TILE]
+        gvec[2:3, lanes] = column_sum(dq.astype(F32))
+        gvec[3:4, lanes] = column_sum(dv.astype(F32))
         both[:, 0:128], both[:, 128:256], both[:, 256:384] = dq, dk, dv
-        scatter_rows(h1t, both, raw_in, p % 2, pl.multiple_of((p // 2) * TILE, 128))
-        plan = (
-            (ro.r1,),
-            (rq0.r0, ru0.r3, ru1.r2),
-            (rq0.r1, ro.r2, ru0.r4),
-            (rq1.r0, rq0.r2, ru1.r3, ro.r3),
-            (rq1.r1, ru0.r5, rd.r2, ru1.r4),
-            (rq2.r0, rq0.r3, rq1.r2, ro.r4, rd.r3),
-        )
-        follow(dict(enumerate(plan)), p)
+
+    def attend_back(j, c):
+        for now, before, p in ((part, other, 2 * j), (other, part, 2 * j + 1)):
+            pair_back(p, now)
+            weight_gradient((p + 5) % 6, before)
+            plan = (
+                (rd.r3, ru0.r2, ro.r1),
+                (),
+                (rq0.r0, rd.r4, ru1.r2),
+                (rq0.r1, ru0.r3, ro.r2, rd.r5),
+                (rq1.r0, ru0.r4, ru1.r3),
+                (rq1.r1, rq0.r2, ro.r3, ru0.r5),
+            )
+            follow(dict(enumerate(plan)), p)
         return c
 
-    lax.fori_loop(0, 6, attend_back, 0)
+    lax.fori_loop(0, 3, attend_back, 0)
+    weight_gradient(5, other)
+    rq2.r0()
+    ru1.r4()
 
     rq2.r1()
     dh2[...] = nt(joint[...], w_in[...])
@@ -947,11 +852,8 @@
         small[1, y, z, x] = jnp.broadcast_to(hidden[f : f + 1], (16, SMALL)).astype(BF)
     rv.r0()
     rq2.r2()
-    rd.r4()
-    rq0.r4()
-    rq1.r3()
-    ru1.r5()
-    ro.r5()
+    rq1.r2()
+    rq0.r3()
     rv.r1()
     rv.r2()
 
@@ -963,14 +865,19 @@
     lax.fori_loop(0, 4, row_blocks(4, back_one), 0)
     grad_copy = pltpu.make_async_copy(dh2, input_grad, ls.at[9])
     grad_copy.start()
+    ro.r4()
     rq2.r3()
-    rq1.r4()
-    rq0.r5()
+    rq1.r3()
     rv.r3()
+    ru1.r5()
+    rq0.r4()
     for t in range(4):
         activate(pre.at[:, t * D : (t + 1) * D], t)
     rq2.r4()
     rv.r4()
+    rq1.r4()
+    rq0.r5()
+    ro.r5()
 
     def result(t, c):
         columns = pl.ds(pl.multiple_of(t * 256, 256), 256)
@@ -989,7 +896,7 @@
         )
     ]
     for r, c in zip(sums, hand):
-        (r.r5 if r is rd else r.r6)()
+        r.r6()
         c.start()
 
     for r in sums:
@@ -1013,8 +920,7 @@
     for h in range(2):
         d_up[:, h * 1536 : h * 1536 + 768] = up0[h]
         d_up[:, h * 1536 + 768 : h * 1536 + 1536] = up1[h]
-        for q in range(2):
-            d_down[48 * q : 48 * q + 48, h * TILE : (h + 1) * TILE] = down[h, q]
+        d_down[:, h * TILE : (h + 1) * TILE] = down[h]
         d_out[:, h * TILE : (h + 1) * TILE] = out[h]
         for k, part in enumerate((in0, in1, in2)):
             for j in range(3):
@@ -1067,15 +973,14 @@
         pltpu.VMEM((1, FF), F32),
         pltpu.VMEM((16, D), F32),
         pltpu.VMEM((1, FF), F32),
-        pltpu.SemaphoreType.DMA((18,)),
-        pltpu.SemaphoreType.DMA((4, 23)),
-        pltpu.SemaphoreType.DMA((4, 23)),
-        pltpu.SemaphoreType.DMA((8, 25)),
-        pltpu.SemaphoreType.DMA((8, 25)),
+        pltpu.SemaphoreType.DMA((29,)),
+        pltpu.SemaphoreType.DMA((5, 23)),
+        pltpu.SemaphoreType.DMA((5, 23)),
+        pltpu.SemaphoreType.DMA((8, 17)),
+        pltpu.SemaphoreType.DMA((8, 17)),
     ]
-    for rows, half in ((24, 768), (24, 768), (24, 384), (24, 384), (24, 384), (24, 384), (16, SMALL)):
+    for rows, half in ((24, 768), (24, 768), (24, 384), (24, 384), (24, 384), (24, 384), (16, SMALL), (96, 384)):
         scratch += reduce_scratch(rows, half)
-    scratch += reduce_z_scratch(96, 384)
     shape = jax.ShapeDtypeStruct
     large = [
         shape((ROWS, D), BF),
@@ -1090,7 +995,7 @@
         up_bias,
     )
     halves = [shape((2, 24, 768), F32)] * 2 + [shape((2, 24, 384), F32)] * 4
-    halves += [shape((2, 16, SMALL), F32), shape((2, 2, 48, 384), F32)]
+    halves += [shape((2, 16, SMALL), F32), shape((2, 96, 384), F32)]
     results = pl.pallas_call(
         kernel,
         out_shape=[*large[:2], *halves],

time: 139 us -> 135 us (0.971)
  Pallas kernels: 137 us -> 133 us
    pallas_call x1, Pallas kernels: 132 us -> 128 us  [shards(): pl.pallas_call(kernel, out_shape=[*large[:2], *halves], in_specs=[hbm, sm...]
where the time goes in v5:
time: 135 us; the launch traced here: 134 us
  Pallas kernels  133 us (99%)
  between operations  1.47 us (1%)
    pallas_call x1, Pallas kernels, shards(): pl.pallas_call(kernel, out_shape=[*large[:2], *halves], in_specs=[hbm, sm...  128 us
    pallas_call x1, Pallas kernels, shards(): pl.pallas_call(finish, out_shape=[*large, *[shape((1, v.shape[0]), F32) f...  5.02 us

profile of v5, /device:TPU:1, one launch (start us, length us, event | category | flops | bytes accessed | tf_op | source)
XLA Modules:
  0.0 134.3 jit_solution(2835457033412171716)
XLA Ops:
  1.3 127.9 %shard_map.280 = (bf16[512,768]{1,0:T(8,128)(2,1)}, f32[512,768]{1,0:T(8,128)}, f32[2,24,768]{2,1,0:T(8,128)}, f32[2,24,768]{2,1,0:T(8,128)}, f32[2,24,384]{2,1,...) custom-call(bf16[512,768]{1,0:T(8,128)(2,1)} %tokens_in.1, ...), custom_call_target="tpu_custom_call" | custom-call | flops 24999999488 | bytes 6000000 | tf_op jit(solution)/shard_map/pallas_call | solution.py:999
  129.2 5.0 %shard_map.281 = (bf16[512,768]{1,0:T(8,128)(2,1)}, f32[512,768]{1,0:T(8,128)}, f32[24,2304]{1,0:T(8,128)}, f32[24,768]{1,0:T(8,128)}, f32[24,3072]{1,0:T(8,128)...) custom-call(bf16[512,768]{1,0:T(8,128)(2,1)} %get-tuple-element.40.l, ...), custom_call_target="tpu_custom_call" | custom-call | tf_op jit(solution)/shard_map/pallas_call | solution.py:1013
